TPU v7x, 32 devices: a whole 2x2x4 slice. The times are simulated.
32 devices in a mesh: seq: 8 (over y, x, core), ch: 4 (over z).
Axes of the slice: x: 2, y: 2, z: 4, core: 2. Of those that a mesh axis runs over, the one named last changes fastest.
Arguments:
- token_ids: int32 [1024], P('seq'), may hold values from 0 to 511
- embedding: bfloat16 [512, 4096], P(None, 'ch'), may hold values from -6 to 6
- short_filter: float32 [7, 4096], P(None, 'ch'), may hold values from -2 to 2
- medium_filter: float32 [128, 4096], P(None, 'ch'), may hold values from -0.5 to 0.5
- long_residue: float32 [16, 4096], P(None, 'ch'), may hold values from -10.5 to 10.5, as said below
- long_rate: float32 [16, 4096], P(None, 'ch'), may hold values from 1e-05 to 0.05
- query_gain: float32 [4096], P('ch'), may hold values from -14 to 14
- key_gain: float32 [4096], P('ch'), may hold values from -14 to 14
Outputs:
- hyena_out: bfloat16 [1024, 4096], P('seq', 'ch')
- attended: bfloat16 [1024, 4096], P('seq', 'ch')
Inputs may be any that keep to these rules, and one draw needn't show every extreme that they name: `long_residue`: residues of the long filter's modes.
All inputs are finite; a program needn't handle non-finite values.
Results may differ from a plain program's by a relative error of at most 0.0095.
The roundings to bfloat16 on the way count: a program that leaves them out, or rounds other values in their place, can miss the bound.
Values may be sent and summed in bfloat16 or wider, within the bound.
No kernel may reach another device: no remote copies, remote signals or barrier semaphores. Data moves between devices by JAX's collectives and lax.ppermute only.
A program may use at most 64 MiB of HBM per device.

v0:
```python
import functools
import math

import jax
import jax.numpy as jnp
import ml_dtypes
import numpy as np
from jax import lax
from jax.experimental import pallas as pl
from jax.experimental.pallas import tpu as pltpu
from jax.sharding import PartitionSpec as P

C = 4096
HEAD = 128


def shifted(value, axis, steps):
    count = lax.axis_size(axis)
    leading, last = (max(0, -steps), min(count, count - steps))
    return lax.ppermute(value, axis, [(source, source + steps) for source in range(leading, last)])


def swapped(shard, axis, apart):
    return lax.ppermute(shard, axis, [(i, i ^ 1 << apart) for i in range(lax.axis_size(axis))])


def from_behind(shard, axis, by):
    size = lax.axis_size(axis)
    return lax.ppermute(shard, axis, [(i, (i + by) % size) for i in range(size)])


def rounded(value):
    return lax.optimization_barrier(value.astype(jnp.bfloat16))


def depthwise_conv(widened, tap_weights, row_count):
    tap_count = tap_weights.shape[0]

    def add_tap(tap_index, running):
        window = lax.dynamic_slice_in_dim(widened, tap_count - 1 - tap_index, row_count, 0)
        return running + tap_weights[tap_index] * window.astype(jnp.float32)

    return lax.fori_loop(
        0, tap_count, add_tap, jnp.zeros((row_count, widened.shape[1]), jnp.float32)
    )


def long_kernel_rows(residue_mine, rate_mine, length):
    positions = jnp.arange(length, dtype=jnp.int32).astype(jnp.float32)
    mode_total = rate_mine.shape[0]

    def add_mode(mode_index, running):
        decay_rate = rate_mine[mode_index]
        mode_weight = (
            residue_mine[mode_index]
            * jnp.sqrt(-jnp.expm1(-2.0 * decay_rate))
            / math.sqrt(mode_total)
        )
        return running + mode_weight[:, None] * jnp.exp(-decay_rate[:, None] * positions[None, :])

    return lax.fori_loop(
        0, mode_total, add_mode, jnp.zeros((rate_mine.shape[1], length), jnp.float32)
    )


def dft_tables(row_size, column_size, period_size):
    row_index = lax.broadcasted_iota(jnp.int32, (row_size, column_size), 0)
    column_index = lax.broadcasted_iota(jnp.int32, (row_size, column_size), 1)
    angles = (row_index * column_index % period_size).astype(jnp.float32) * (
        2.0 * math.pi / period_size
    )
    return (jnp.cos(angles), jnp.sin(angles))


def forward_dft(signal, outer_size, inner_size):
    highest = lax.Precision.HIGHEST
    cos_outer, sin_outer = dft_tables(outer_size // 2, outer_size, outer_size)
    twiddle_cos, twiddle_sin = dft_tables(outer_size, inner_size, outer_size * inner_size)
    cos_inner, sin_inner = dft_tables(inner_size, inner_size, inner_size)
    step_real = jnp.einsum("pab,ak->pkb", signal, cos_outer, precision=highest)
    step_imag = -jnp.einsum("pab,ak->pkb", signal, sin_outer, precision=highest)
    turned_real = step_real * twiddle_cos + step_imag * twiddle_sin
    turned_imag = step_imag * twiddle_cos - step_real * twiddle_sin
    spec_real = jnp.einsum("pkb,bm->pkm", turned_real, cos_inner, precision=highest) + jnp.einsum(
        "pkb,bm->pkm", turned_imag, sin_inner, precision=highest
    )
    spec_imag = jnp.einsum("pkb,bm->pkm", turned_imag, cos_inner, precision=highest) - jnp.einsum(
        "pkb,bm->pkm", turned_real, sin_inner, precision=highest
    )
    return (spec_real, spec_imag)


def inverse_dft(spec_real, spec_imag, outer_size, inner_size):
    highest = lax.Precision.HIGHEST
    cos_outer, sin_outer = dft_tables(outer_size // 2, outer_size, outer_size)
    twiddle_cos, twiddle_sin = dft_tables(outer_size, inner_size, outer_size * inner_size)
    cos_inner, sin_inner = dft_tables(inner_size, inner_size, inner_size)
    back_real = jnp.einsum("pkm,mb->pkb", spec_real, cos_inner, precision=highest) - jnp.einsum(
        "pkm,mb->pkb", spec_imag, sin_inner, precision=highest
    )
    back_imag = jnp.einsum("pkm,mb->pkb", spec_real, sin_inner, precision=highest) + jnp.einsum(
        "pkm,mb->pkb", spec_imag, cos_inner, precision=highest
    )
    turned_real = back_real * twiddle_cos - back_imag * twiddle_sin
    turned_imag = back_real * twiddle_sin + back_imag * twiddle_cos
    signal = jnp.einsum("pkb,ak->pab", turned_real, cos_outer, precision=highest) - jnp.einsum(
        "pkb,ak->pab", turned_imag, sin_outer, precision=highest
    )
    return signal / (outer_size * inner_size)


def attend_block(query_rows, query_index, key_block, value_block, key_start, running, score_scale):
    row_peak, row_total, blended = running
    scores = (
        jnp.einsum("qhd,khd->hqk", query_rows, key_block, preferred_element_type=jnp.float32)
        * score_scale
    )
    key_index = key_start + jnp.arange(key_block.shape[0], dtype=jnp.int32)
    scores = jnp.where(key_index[None, None, :] <= query_index[None, :, None], scores, -1e30)
    new_peak = jnp.maximum(row_peak, jnp.max(scores, axis=2))
    weights = jnp.exp(scores - new_peak[:, :, None])
    rescale = jnp.exp(row_peak - new_peak)
    row_total = row_total * rescale + jnp.sum(weights, axis=2)
    blended = blended * rescale[:, :, None] + jnp.einsum(
        "hqk,khd->hqd",
        weights.astype(jnp.bfloat16),
        value_block,
        preferred_element_type=jnp.float32,
    )
    return (new_peak, row_total, blended)


def merge_partials(first_part, second_part):
    peak_one, total_one, blend_one = first_part
    peak_two, total_two, blend_two = second_part
    new_peak = jnp.maximum(peak_one, peak_two)
    scale_one = jnp.exp(peak_one - new_peak)
    scale_two = jnp.exp(peak_two - new_peak)
    new_total = total_one * scale_one + total_two * scale_two
    new_blend = blend_one * scale_one[..., None] + blend_two * scale_two[..., None]
    return (new_peak, new_total, new_blend)


def split_halves(stacked_part, half_size, upper_side):
    lower_half = stacked_part[:, :half_size]
    upper_half = stacked_part[:, half_size:]
    keep_half = jnp.where(upper_side == 1, upper_half, lower_half)
    send_half = jnp.where(upper_side == 1, lower_half, upper_half)
    return (keep_half, send_half)


def by_position(
    token_ids, embedding, short_filter, medium_filter, long_residue, long_rate, query_gain, key_gain
):
    tok_count = token_ids.shape[0]
    vocab_size = embedding.shape[0]
    width_dev = embedding.shape[1]
    seq_count = lax.axis_size("seq")
    seq_index = lax.axis_index("seq")
    one_hot = (
        token_ids[:, None] == lax.broadcasted_iota(jnp.int32, (tok_count, vocab_size), 1)
    ).astype(jnp.bfloat16)
    embedded = jnp.dot(one_hot, embedding, preferred_element_type=jnp.float32).astype(jnp.bfloat16)
    short_taps = short_filter.shape[0]
    rim_rows = shifted(embedded[tok_count - (short_taps - 1) :], "seq", 1)
    widened = jnp.concatenate([rim_rows, embedded], axis=0)
    short_part = depthwise_conv(widened, short_filter, tok_count)
    short_gated = rounded(embedded.astype(jnp.float32) * short_part)
    medium_taps = medium_filter.shape[0]
    upper_rows = shifted(short_gated[tok_count - (medium_taps - 1) :], "seq", 1)
    widened_two = jnp.concatenate([upper_rows, short_gated], axis=0)
    medium_part = depthwise_conv(widened_two, medium_filter, tok_count)
    medium_gated = rounded(short_gated.astype(jnp.float32) * medium_part)
    per_dev = width_dev // seq_count
    length = tok_count * seq_count
    grouped = medium_gated.T.reshape(seq_count, per_dev, tok_count)
    spread = lax.all_to_all(grouped, "seq", split_axis=0, concat_axis=2, tiled=True).reshape(
        per_dev, length
    )
    rate_mine = lax.dynamic_slice_in_dim(long_rate, seq_index * per_dev, per_dev, 1)
    residue_mine = lax.dynamic_slice_in_dim(long_residue, seq_index * per_dev, per_dev, 1)
    kernel = long_kernel_rows(residue_mine, rate_mine, length)
    outer_size = 128
    inner_size = 2 * length // outer_size
    spread_float = spread.astype(jnp.float32)
    data_real, data_imag = forward_dft(
        spread_float.reshape(per_dev, outer_size // 2, inner_size), outer_size, inner_size
    )
    kernel_real, kernel_imag = forward_dft(
        kernel.reshape(per_dev, outer_size // 2, inner_size), outer_size, inner_size
    )
    product_real = data_real * kernel_real - data_imag * kernel_imag
    product_imag = data_real * kernel_imag + data_imag * kernel_real
    long_part = inverse_dft(product_real, product_imag, outer_size, inner_size).reshape(
        per_dev, length
    )
    channel_out = (spread_float * long_part).astype(jnp.bfloat16)
    returned = lax.all_to_all(channel_out[None], "seq", split_axis=2, concat_axis=0, tiled=True)
    hyena_out = returned.reshape(width_dev, tok_count).T
    head_count = width_dev // HEAD
    hyena_float = hyena_out.astype(jnp.float32)
    square_sums = jnp.sum(hyena_float * hyena_float, axis=1)
    total_sums = lax.psum(square_sums, "ch")
    inverse_scale = lax.rsqrt(total_sums / C + 1e-05)
    normed = hyena_float * inverse_scale[:, None]
    values = normed.astype(jnp.bfloat16).reshape(tok_count, head_count, HEAD)
    queries = (
        (normed * query_gain[None, :]).astype(jnp.bfloat16).reshape(tok_count, head_count, HEAD)
    )
    key_rows = (
        (normed * key_gain[None, :]).astype(jnp.bfloat16).reshape(tok_count, head_count, HEAD)
    )
    group_size = 2
    level_count = group_size.bit_length() - 1
    seq_bits = seq_count.bit_length() - 1
    base_bit = seq_bits - level_count
    stride = seq_count // group_size
    stacked = queries[None]
    level = 0
    bit_number = base_bit + level
    partner_rows = swapped(stacked, "seq", bit_number)
    upper_side = seq_index >> bit_number & 1
    stacked = jnp.where(
        upper_side == 1,
        jnp.concatenate([partner_rows, stacked], axis=0),
        jnp.concatenate([stacked, partner_rows], axis=0),
    )
    query_rows = stacked.reshape(group_size * tok_count, head_count, HEAD)
    group_first = seq_index % stride
    block_numbers = group_first + stride * jnp.arange(group_size, dtype=jnp.int32)
    query_index = (
        block_numbers[:, None] * tok_count + jnp.arange(tok_count, dtype=jnp.int32)[None, :]
    ).reshape(group_size * tok_count)
    score_scale = HEAD ** (-0.5)
    partial_state = (
        jnp.full((head_count, group_size * tok_count), -1e30, jnp.float32),
        jnp.zeros((head_count, group_size * tok_count), jnp.float32),
        jnp.zeros((head_count, group_size * tok_count, HEAD), jnp.float32),
    )

    def cycle_step(turn_number, carried):
        key_block, value_block, running = carried
        key_block, value_block = from_behind((key_block, value_block), "seq", -1)
        source_block = jnp.remainder(seq_index + turn_number, seq_count)
        running = attend_block(
            query_rows,
            query_index,
            key_block,
            value_block,
            source_block * tok_count,
            running,
            score_scale,
        )
        return (key_block, value_block, running)

    carried = lax.fori_loop(1, stride + 1, cycle_step, (key_rows, values, partial_state))
    row_peak, row_total, blended = carried[2]
    row_peak = row_peak.reshape(head_count, group_size, tok_count)
    row_total = row_total.reshape(head_count, group_size, tok_count)
    blended = blended.reshape(head_count, group_size, tok_count, HEAD)
    for level in reversed(range(level_count)):
        bit_number = base_bit + level
        half_size = row_peak.shape[1] // 2
        upper_side = seq_index >> bit_number & 1
        keep_peak, send_peak = split_halves(row_peak, half_size, upper_side)
        keep_total, send_total = split_halves(row_total, half_size, upper_side)
        keep_blend, send_blend = split_halves(blended, half_size, upper_side)
        got_peak, got_total, got_blend = swapped(
            (send_peak, send_total, send_blend), "seq", bit_number
        )
        row_peak, row_total, blended = merge_partials(
            (keep_peak, keep_total, keep_blend), (got_peak, got_total, got_blend)
        )
    normalized = blended[:, 0] / row_total[:, 0][:, :, None]
    attended = normalized.transpose(1, 0, 2).reshape(tok_count, width_dev).astype(jnp.bfloat16)
    return (hyena_out, attended)


def transform_tables(block):
    size = 2 * block
    step = 2.0 * np.pi / size
    freq = (np.arange(block) + 0.5)[:, None]
    angle = freq * np.arange(size)[None, :] * step
    forward = np.concatenate([np.cos(angle), -np.sin(angle)], axis=0)
    angle = (np.arange(block)[:, None] + block) * freq.T * step
    backward = np.concatenate([np.cos(angle), -np.sin(angle)], axis=1) * (2.0 / size)

    def parts(table):
        kept = []
        for _ in range(3):
            kept.append(table.astype(np.float32).astype(ml_dtypes.bfloat16))
            table = table - kept[-1].astype(np.float64)
        return np.concatenate(kept, axis=0)

    forward, backward = parts(forward), parts(backward)
    first, second, third = np.split(forward[:, :block], 3)
    taps = np.concatenate([np.concatenate([first, second], axis=1), np.concatenate([first, third], axis=1)], axis=0)
    return forward, backward, taps


def split_pair(value):
    upper = value.astype(jnp.bfloat16)
    return upper, (value - upper.astype(jnp.float32)).astype(jnp.bfloat16)


def split_three(value):
    upper = value.astype(jnp.bfloat16)
    rest = value - upper.astype(jnp.float32)
    middle = rest.astype(jnp.bfloat16)
    return upper, middle, (rest - middle.astype(jnp.float32)).astype(jnp.bfloat16)


def minus_expm1(value):
    term = value
    series = value
    for order in range(2, 11):
        term = term * value * (-1.0 / order)
        series = series + term
    return jnp.where(value < 0.5, series, 1.0 - jnp.exp(-value))


def dot32(left, right):
    return jnp.dot(left, right, preferred_element_type=jnp.float32)


def far_first(count):
    return [0, *range(count - 1, 0, -1)]


def own_lanes(width):
    return pl.ds(pl.multiple_of(lax.axis_index("seq") * width, width), width)


def fetch_kernel(
    token_ids, residue, rate, medium, table, ids_out, residue_out, rate_out, medium_out, table_out, sems
):
    lanes = own_lanes(medium_out.shape[1])
    copies = [
        pltpu.make_async_copy(source, target, sems.at[i])
        for i, (source, target) in enumerate(
            [
                (token_ids, ids_out),
                (residue.at[:, lanes], residue_out),
                (rate.at[:, lanes], rate_out),
                (medium.at[:, lanes], medium_out),
                (table, table_out),
            ]
        )
    ]
    for copy in copies:
        copy.start()
    for copy in copies:
        copy.wait()


def response_kernel(residue, rate, medium, table, medium_out, long_out):
    block, width = medium.shape
    size = 2 * block
    mode_total = rate.shape[0]
    block_total = long_out.shape[1] // width

    def transformed(signal):
        up, middle, low = split_three(signal)
        return (
            dot32(table[0:size, :], jnp.concatenate([up, up], axis=0))
            + dot32(table[0:size, :], jnp.concatenate([middle, middle], axis=0))
            + dot32(table[size : 2 * size, :], jnp.concatenate([low, up], axis=0))
        )

    medium_out[...] = transformed(medium[...])
    decays = rate[...]
    weights = residue[...] * jnp.sqrt(minus_expm1(2.0 * decays)) / math.sqrt(mode_total)
    modes = [weights * jnp.exp(-decays * float(part * block)) for part in range(block_total)]
    place = lax.broadcasted_iota(jnp.int32, (block, width), 0).astype(jnp.float32)
    rows = 32
    tiles = []
    for first in range(0, block, rows):
        sums = [jnp.zeros((rows, width), jnp.float32) for _ in range(block_total)]
        for mode in range(mode_total):
            shape = jnp.exp(-decays[mode : mode + 1, :] * place[first : first + rows])
            for part in range(block_total):
                sums[part] = sums[part] + modes[part][mode : mode + 1, :] * shape
        tiles.append(jnp.concatenate(sums, axis=1))
    long_out[...] = transformed(jnp.concatenate(tiles, axis=0))


def conv_kernel(*refs, piece_count):
    pieces = refs[:piece_count]
    (embedding, short, medium_resp, long_resp, forward, backward, hyena, sums) = refs[piece_count : piece_count + 8]
    ids, ordered, padded, row_sums = refs[piece_count + 8 :]
    width = padded.shape[1]
    block = width
    size = 2 * block
    length = hyena.shape[0]
    count = length // block
    pair = count // 2
    me = lax.axis_index("seq")
    for i, piece in zip(far_first(piece_count), pieces):
        ids[2 * i : 2 * i + 2, :] = piece[...]
    for b in range(count):
        ordered[b : b + 1, :] = ids[pl.ds(lax.bitwise_xor(me, b), 1), :]
    across = jnp.transpose(ordered[...].astype(jnp.float32), (1, 0)).astype(jnp.int32)
    padded[0:8, :] = jnp.zeros((8, width), jnp.float32)
    table = embedding[:, own_lanes(width)]
    short_taps = short[:, own_lanes(width)]
    vocab = table.shape[0]
    entries = lax.broadcasted_iota(jnp.int32, (block, vocab), 1)
    rows = 16

    def embed(chunk):
        for b in range(chunk * pair, (chunk + 1) * pair):
            chosen = jnp.where(across[:, b : b + 1] == entries, 1.0, 0.0).astype(jnp.bfloat16)
            padded[8 + b * block : 8 + (b + 1) * block, :] = dot32(chosen, table)

    nothing = jnp.zeros((block, width), jnp.bfloat16)
    gated = [{-1: nothing}, {-1: nothing}]
    spectra, products = [{}, {}], [{}, {}]

    def short_gate(chunk):
        for b in range(chunk * pair, (chunk + 1) * pair):
            running = jnp.zeros((block, width), jnp.float32)
            for j in range(short_taps.shape[0]):
                running = running + short_taps[j : j + 1, :] * padded[8 + b * block - j : 8 + (b + 1) * block - j, :]
            signal = padded[8 + b * block : 8 + (b + 1) * block, :] * running
            gated[0][b] = signal.astype(jnp.bfloat16)

    def analyse(turn, chunk):
        span = range(chunk * pair, (chunk + 1) * pair)
        signal = jnp.concatenate(
            [jnp.concatenate([gated[turn][b - 1] for b in span], axis=1)]
            + [jnp.concatenate([gated[turn][b] for b in span], axis=1)],
            axis=0,
        )
        spectrum = (
            dot32(forward[0:size, :], signal)
            + dot32(forward[size : 2 * size, :], signal)
            + dot32(forward[2 * size : 3 * size, :], signal)
        )
        for i, b in enumerate(span):
            spectra[turn][b] = spectrum[:, i * width : (i + 1) * width]

    def multiply(turn, response, chunk):
        columns = []
        for b in range(chunk * pair, (chunk + 1) * pair):
            tiles = [[], []]
            for first in range(0, block, rows):
                upper = slice(first, first + rows)
                lower = slice(block + first, block + first + rows)
                total_real, total_imag = 0.0, 0.0
                for part in range(b + 1 if turn else 1):
                    taps = slice(part * width, (part + 1) * width)
                    real, imag = spectra[turn][b - part][upper], spectra[turn][b - part][lower]
                    filt_real, filt_imag = response[upper, taps], response[lower, taps]
                    total_real = total_real + (real * filt_real - imag * filt_imag)
                    total_imag = total_imag + (real * filt_imag + imag * filt_real)
                tiles[0].append(split_three(total_real))
                tiles[1].append(split_three(total_imag))
            columns.append([jnp.concatenate([tile[i] for tile in tiles[0] + tiles[1]], axis=0) for i in range(3)])
        products[turn][chunk] = [jnp.concatenate([column[i] for column in columns], axis=1) for i in range(3)]

    def synthesise(turn, chunk):
        up, middle, low = products[turn].pop(chunk)
        first, second, third = [backward[i * block : (i + 1) * block, :] for i in range(3)]
        return (
            dot32(first, up)
            + (dot32(second, up) + dot32(first, middle))
            + (dot32(third, up) + dot32(second, middle) + dot32(first, low))
        )

    def gate(turn, chunk):
        out = synthesise(turn, chunk)
        results = []
        for i in range(pair):
            past = gated[turn][chunk * pair + i].astype(jnp.float32)
            results.append((past * out[:, i * width : (i + 1) * width]).astype(jnp.bfloat16))
        return results

    def medium_gate(chunk):
        for i, signal in enumerate(gate(0, chunk)):
            gated[1][chunk * pair + i] = signal

    ones = jnp.ones((size, width), jnp.bfloat16)
    diagonal = lax.broadcasted_iota(jnp.int32, (block, block), 0) == lax.broadcasted_iota(
        jnp.int32, (block, block), 1
    )

    def long_gate(chunk):
        for i, result in enumerate(gate(1, chunk)):
            b = chunk * pair + i
            hyena[b * block : (b + 1) * block, :] = result
            wide = result.astype(jnp.float32)
            spread = dot32(jnp.concatenate(split_pair(wide * wide), axis=1), ones)
            row_sums[b : b + 1, :] = jnp.sum(jnp.where(diagonal, spread, 0.0), axis=0, keepdims=True)

    stages = [
        embed,
        short_gate,
        functools.partial(analyse, 0),
        functools.partial(multiply, 0, medium_resp),
        medium_gate,
        functools.partial(analyse, 1),
        functools.partial(multiply, 1, long_resp),
        long_gate,
    ]
    chunks = count // pair
    for turn in range(chunks + len(stages) - 1):
        for stage in range(len(stages)):
            if 0 <= turn - stage < chunks:
                stages[stage](turn - stage)
    sums[...] = row_sums[...]


def attend_kernel(own, other, sums, query_gain, key_gain, out, queries, keys, values, *, channel_count):
    length, width = own.shape
    count = sums.shape[1]
    block = length // count
    me = lax.axis_index("seq")
    core = lax.rem(me, 2)
    total = jnp.sum(sums[...], axis=0)
    inverse = lax.rsqrt(total / channel_count + 1e-05)
    inverse = jnp.transpose(inverse, (1, 0))
    signals = (own, other)
    gains = []
    for side in range(2):
        lanes = pl.ds(pl.multiple_of(lax.bitwise_xor(me, side) * width, width), width)
        gains.append((query_gain[0:1, lanes], key_gain[0:1, lanes]))

    def normalise(b):
        spans = slice(b * block, (b + 1) * block)
        scale = jnp.broadcast_to(inverse[:, b : b + 1], (block, width))
        for side, signal in enumerate(signals):
            normed = signal[spans, :].astype(jnp.float32) * scale
            values[side, spans, :] = normed.astype(jnp.bfloat16)
            keys[side, spans, :] = (normed * gains[side][1]).astype(jnp.bfloat16)
            queries[side, spans, :] = (normed * gains[side][0]).astype(jnp.bfloat16)

    row_index = lax.broadcasted_iota(jnp.int32, (block, 2 * block), 0) + core * block
    allowed = lax.broadcasted_iota(jnp.int32, (block, 2 * block), 1) <= row_index

    def score(chip, side):
        reach = (chip + 1) * 2 * block
        start = pl.multiple_of((2 * chip + core) * block, block)
        scores = lax.dot_general(
            queries[side, pl.ds(start, block), :],
            keys[side, 0:reach, :],
            (((1,), (1,)), ((), ())),
            preferred_element_type=jnp.float32,
        )
        last = jnp.where(allowed, scores[:, reach - 2 * block :], -1e30)
        return jnp.concatenate([scores[:, : reach - 2 * block], last], axis=1) if chip else last

    def weigh(scores):
        peak = jnp.max(scores, axis=1, keepdims=True)
        weights = jnp.exp2((scores - peak) * (width**-0.5 * math.log2(math.e)))
        return weights.astype(jnp.bfloat16), jnp.sum(weights, axis=1, keepdims=True)

    def blend(chip, side, weights, row_total):
        reach = (chip + 1) * 2 * block
        start = pl.multiple_of((2 * chip + core) * block, block)
        place = lax.bitwise_xor(me // 2, chip)
        half = lax.bitwise_xor(core, side)
        blended = dot32(weights, values[side, 0:reach, :])
        lanes = pl.ds(pl.multiple_of(half * width, width), width)
        out[place, :, lanes] = (blended / row_total).astype(jnp.bfloat16)
        lanes = pl.ds(pl.multiple_of((2 + half) * width, width), width)
        out[place, :, lanes] = signals[side][pl.ds(start, block), :]

    for b in range(count):
        normalise(b)
    chains = [(chip, side) for chip in range(count // 2) for side in range(2)]
    scored, weighed = {}, {}
    for turn in range(len(chains) + 2):
        if turn < len(chains):
            scored[turn] = score(*chains[turn])
        if 0 <= turn - 1 < len(chains):
            weighed[turn - 1] = weigh(scored.pop(turn - 1))
        if 0 <= turn - 2 < len(chains):
            blend(*chains[turn - 2], *weighed.pop(turn - 2))


def place_kernel(*refs):
    blocks, (hyena, attended) = refs[:-2], refs[-2:]
    span = blocks[0].shape[1] // 2
    chip = lax.axis_index("seq") // 2
    for i, block in zip(far_first(len(blocks)), blocks):
        lanes = pl.ds(pl.multiple_of(lax.bitwise_xor(chip, i) * span, span), span)
        attended[:, lanes] = block[:, 0:span]
        hyena[:, lanes] = block[:, span : 2 * span]


def by_head(
    token_ids, embedding, short_filter, medium_filter, long_residue, long_rate, query_gain, key_gain
):
    seq_count = lax.axis_size("seq")
    ch_count = lax.axis_size("ch")
    block = token_ids.shape[0]
    width_dev = embedding.shape[1]
    length = block * seq_count
    width = HEAD
    f32, bf16 = jnp.float32, jnp.bfloat16
    forward, backward, tap_table = transform_tables(block)
    whole = pl.BlockSpec(memory_space=pltpu.VMEM)
    params = pltpu.CompilerParams(vmem_limit_bytes=24 * 1024 * 1024)

    def exchange(value, apart):
        return lax.ppermute(value, "seq", [(i, i ^ apart) for i in range(seq_count)])

    mode_total = long_rate.shape[0]
    in_hbm = pl.BlockSpec(memory_space=pltpu.HBM)

    def fetched(value):
        return pltpu.with_memory_space_constraint(value, pltpu.HBM)

    partner_ids = exchange(token_ids, 1)
    operands = (token_ids, long_residue, long_rate, medium_filter, jnp.asarray(tap_table))
    own_ids, *filters = pl.pallas_call(
        fetch_kernel,
        out_shape=[
            jax.ShapeDtypeStruct((block,), jnp.int32),
            jax.ShapeDtypeStruct((mode_total, width), f32),
            jax.ShapeDtypeStruct((mode_total, width), f32),
            jax.ShapeDtypeStruct((block, width), f32),
            jax.ShapeDtypeStruct(tap_table.shape, bf16),
        ],
        in_specs=[in_hbm] * 5,
        out_specs=[whole] * 5,
        scratch_shapes=[pltpu.SemaphoreType.DMA((5,))],
        compiler_params=params,
        cost_estimate=pl.CostEstimate(flops=10**9, bytes_accessed=2 * 10**6, transcendentals=0),
        name="fetched_operands",
    )(*[fetched(value) for value in operands])
    chip_ids = jnp.stack([own_ids, partner_ids])
    pieces = [chip_ids] + [exchange(chip_ids, 2 * i) for i in far_first(seq_count // 2)[1:]]
    medium_resp, long_resp = pl.pallas_call(
        response_kernel,
        out_shape=[
            jax.ShapeDtypeStruct((2 * block, width), f32),
            jax.ShapeDtypeStruct((2 * block, length), f32),
        ],
        in_specs=[whole] * 4,
        out_specs=[whole] * 2,
        compiler_params=params,
        cost_estimate=pl.CostEstimate(flops=2 * 10**9, bytes_accessed=2 * 10**6, transcendentals=3 * 10**5),
        name="filter_responses",
    )(*filters)

    hyena, square_sums = pl.pallas_call(
        functools.partial(conv_kernel, piece_count=len(pieces)),
        out_shape=[
            jax.ShapeDtypeStruct((length, width), bf16),
            jax.ShapeDtypeStruct((seq_count, block), f32),
        ],
        in_specs=[whole] * (len(pieces) + 6),
        out_specs=[whole, whole],
        scratch_shapes=[
            pltpu.VMEM((seq_count, block), jnp.int32),
            pltpu.VMEM((seq_count, block), jnp.int32),
            pltpu.VMEM((8 + length, width), f32),
            pltpu.VMEM((seq_count, block), f32),
        ],
        compiler_params=params,
        cost_estimate=pl.CostEstimate(flops=2 * 10**9, bytes_accessed=2 * 10**6, transcendentals=0),
        name="gated_convolutions",
    )(*pieces, embedding, short_filter, medium_resp, long_resp, forward, backward)

    other = exchange(hyena, 1)
    devices = seq_count * ch_count
    all_sums = lax.all_to_all(
        jnp.broadcast_to(square_sums[None], (devices, seq_count, block)), ("seq", "ch"), 0, 0, tiled=True
    )
    outgoing = pl.pallas_call(
        functools.partial(attend_kernel, channel_count=width_dev * ch_count),
        out_shape=jax.ShapeDtypeStruct((seq_count // 2, block, 4 * width), bf16),
        in_specs=[whole] * 5,
        out_specs=whole,
        scratch_shapes=[pltpu.VMEM((2, length, width), bf16)] * 3,
        compiler_params=params,
        cost_estimate=pl.CostEstimate(flops=2 * 10**9, bytes_accessed=10**6, transcendentals=10**6),
        name="attention",
    )(hyena, other, all_sums, query_gain.reshape(1, width_dev), key_gain.reshape(1, width_dev))
    blocks = [outgoing[0]] + [exchange(outgoing[i], 2 * i) for i in far_first(seq_count // 2)[1:]]
    return pl.pallas_call(
        place_kernel,
        out_shape=[jax.ShapeDtypeStruct((block, width_dev), bf16)] * 2,
        in_specs=[whole] * len(blocks),
        out_specs=[whole, whole],
        compiler_params=params,
        name="placed_blocks",
    )(*blocks)


def on_device(*operands):
    seq_count = lax.axis_size("seq")
    token_ids, embedding, _, medium_filter = operands[:4]
    block = token_ids.shape[0]
    fits = (
        embedding.shape[1] == seq_count * HEAD
        and block == HEAD
        and medium_filter.shape[0] == block
        and seq_count % 8 == 0
        and seq_count & (seq_count - 1) == 0
    )
    return by_head(*operands) if fits else by_position(*operands)


def solution(mesh):
    in_specs = (
        P("seq"),
        P(None, "ch"),
        P(None, "ch"),
        P(None, "ch"),
        P(None, "ch"),
        P(None, "ch"),
        P("ch"),
        P("ch"),
    )
    out_specs = (P("seq", "ch"), P("seq", "ch"))
    return jax.shard_map(
        on_device, mesh=mesh, in_specs=in_specs, out_specs=out_specs, check_vma=False
    )
```

profile of v0, /device:TPU:0, one launch (start us, length us, event | category | flops | bytes accessed | tf_op | source)
XLA Modules:
  0.0 37.4 jit_solution(14236635135942183070)
XLA Ops:
  0.6 0.5 %collective-permute-start = (s32[128]{0:T(128)}, s32[128]{0:T(128)S(1)}, u32[]{:S(2)}, u32[]{:S(2)}) collective-permute-start(s32[128]{0:T(128)} %token_ids.1), channel_id=1, source_target_pairs={{0,4},{4,0},{8,12},{12,8},{16,20},{20,16},{24,28},{28,24},{1,5},{5... | collective-permute-start | bytes 1544 | tf_op jit(solution)/shard_map/ppermute | solution.py:606
  1.1 1.1 %fetched_operands.1 = (s32[128]{0:T(128)S(1)}, f32[16,128]{1,0:T(8,128)S(1)}, f32[16,128]{1,0:T(8,128)S(1)}, f32[128,128]{1,0:T(8,128)S(1)}, bf16[512,256]{1,0:T(8,128)(2,1)S(1)}) custom-call(s32[128]{0:T(128)} %token_ids.1, f32[16,1024]{1,0:T(8,128)} %residue.1, f32[16,1024]{1,0:T(8,128)} %rate.1, f32[128,1024]{1,0:T(8,128)} %medium.1, ...), custom_call_target="tpu_custom_call" | custom-call | flops 1000000000 | bytes 2000000 | tf_op jit(solution)/shard_map/fetched_operands/pallas_call | solution.py:616
  2.2 0.0 collective-permute-done
  2.3 3.6 %collective-permute-start.1 = (s32[2,128]{1,0:T(2,128)S(1)}, s32[2,128]{1,0:T(2,128)S(1)}, u32[]{:S(2)}, u32[]{:S(2)}) collective-permute-start(s32[2,128]{1,0:T(2,128)S(1)} %pad_add_fusion.refs_0_), channel_id=1, source_target_pairs={{0,24},{4,28},{8,16},{12,20},{16,8},{20,12},{24,0},{28,4},{1,25},{... | collective-permute-start | bytes 3080 | tf_op jit(solution)/shard_map/ppermute | solution.py:606
  5.9 0.5 %collective-permute-start.2 = (s32[2,128]{1,0:T(2,128)S(1)}, s32[2,128]{1,0:T(2,128)S(1)}, u32[]{:S(2)}, u32[]{:S(2)}) collective-permute-start(s32[2,128]{1,0:T(2,128)S(1)} %pad_add_fusion.refs_0_), channel_id=1, source_target_pairs={{0,16},{4,20},{8,24},{12,28},{16,0},{20,4},{24,8},{28,12},{1,17},{... | collective-permute-start | bytes 3080 | tf_op jit(solution)/shard_map/ppermute | solution.py:606
  6.4 0.1 collective-permute-start.3
  6.5 0.0 copy-start
  6.5 0.0 copy-start.1
  6.5 0.0 copy-start.4
  6.5 0.0 copy-start.5
  6.5 1.3 %filter_responses.1 = (f32[256,128]{1,0:T(8,128)S(1)}, f32[256,1024]{1,0:T(8,128)S(1)}) custom-call(f32[16,128]{1,0:T(8,128)S(1)} %get-tuple-element.12.residue, f32[16,128]{1,0:T(8,128)S(1)} %get-tuple-element.13.rate, f32[128,128]{1,0:T(8,128)S(1)} %get-tuple-element.14.medium, bf16[512,256]{1,0:T(8,128)(2,1)S(1)} %get-tuple-element.15.table), custom_call_target="tpu_custom_call" | custom-call | flops 2000000000 | bytes 2000000 | tf_op jit(solution)/shard_map/filter_responses/pallas_call | solution.py:634
  7.8 0.0 collective-permute-done.1.refs_1_
  7.9 1.6 %collective-permute-done.2.refs_2_ = s32[2,128]{1,0:T(2,128)S(1)} collective-permute-done((s32[2,128]{1,0:T(2,128)S(1)}, s32[2,128]{1,0:T(2,128)S(1)}, u32[]{:S(2)}, u32[]{:S(2)}) %collective-permute-start.2) | collective-permute-done | bytes 1056 | tf_op jit(solution)/shard_map/ppermute | solution.py:606
  9.4 0.5 %collective-permute-done.3.refs_3_ = s32[2,128]{1,0:T(2,128)S(1)} collective-permute-done((s32[2,128]{1,0:T(2,128)S(1)}, s32[2,128]{1,0:T(2,128)S(1)}, u32[]{:S(2)}, u32[]{:S(2)}) %collective-permute-start.3) | collective-permute-done | bytes 1056 | tf_op jit(solution)/shard_map/ppermute | solution.py:606
  9.9 0.0 copy-done
  9.9 0.0 copy-done.1
  9.9 0.0 copy-done.4
  9.9 0.0 copy-done.5
  10.0 3.4 %gated_convolutions.1 = (bf16[1024,128]{1,0:T(8,128)(2,1)S(1)}, f32[8,128]{1,0:T(8,128)S(1)}) custom-call(s32[2,128]{1,0:T(2,128)S(1)} %pad_add_fusion.refs_0_, s32[2,128]{1,0:T(2,128)S(1)} %collective-permute-done.1.refs_1_, s32[2,128]{1,0:T(2,128)S(1)} %collective-permute-done.2.refs_2_, s32[2,128]{1,0:T(2,128)S(1)} %collective-permute-done.3.refs_3_, ...), custom_call_target="tpu_custom_call" | custom-call | flops 2000000000 | bytes 2000000 | tf_op jit(solution)/shard_map/gated_convolutions/pallas_call | solution.py:647
  13.4 0.1 collective-permute-start.4
  13.5 0.0 copy-start.2
  13.5 0.0 copy-start.3
  13.5 13.2 %all_to_all.5.sums = f32[32,8,128]{2,1,0:T(8,128)S(1)} all-to-all(f32[32,8,128]{2,1,0:T(8,128)S(1)} %broadcast_in_dim.2), channel_id=1, replica_groups=mesh['seq'=8,'ch'=4] {'seq','ch'}, dimensions={0} | all-to-all | bytes 262144 | tf_op jit(solution)/shard_map/all_to_all | solution.py:668
  26.7 0.0 collective-permute-done.4.other
  26.7 0.0 copy-done.2
  26.7 0.0 copy-done.3
  26.7 1.6 %attention.1 = bf16[4,128,512]{2,1,0:T(8,128)(2,1)S(1)} custom-call(bf16[1024,128]{1,0:T(8,128)(2,1)S(1)} %get-tuple-element.18.own, bf16[1024,128]{1,0:T(8,128)(2,1)S(1)} %collective-permute-done.4.other, f32[32,8,128]{2,1,0:T(8,128)S(1)} %all_to_all.5.sums, f32[1,1024]{1,0:T(1,128)S(1)} %bitcast.13, f32[1,1024]{1,0:T(1,128)S(1)} %bitcast.14), custom_call_target="tpu_custom_call" | custom-call | flops 2000000000 | bytes 1000000 | tf_op jit(solution)/shard_map/attention/pallas_call | solution.py:671
  28.4 0.8 %collective-permute-start.5 = (bf16[128,512]{1,0:T(8,128)(2,1)S(1)}, bf16[128,512]{1,0:T(8,128)(2,1)S(1)}, u32[]{:S(2)}, u32[]{:S(2)}) collective-permute-start(bf16[128,512]{1,0:T(8,128)(2,1)S(1)} %get-tuple-element.22), channel_id=1, source_target_pairs={{0,24},{4,28},{8,16},{12,20},{16,8},{20,12},{24,0},{28,4},{1,25},{... | collective-permute-start | bytes 393224 | tf_op jit(solution)/shard_map/ppermute | solution.py:606
  29.2 1.5 %collective-permute-start.6 = (bf16[128,512]{1,0:T(8,128)(2,1)S(1)}, bf16[128,512]{1,0:T(8,128)(2,1)S(1)}, u32[]{:S(2)}, u32[]{:S(2)}) collective-permute-start(bf16[128,512]{1,0:T(8,128)(2,1)S(1)} %get-tuple-element.21), channel_id=1, source_target_pairs={{0,16},{4,20},{8,24},{12,28},{16,0},{20,4},{24,8},{28,12},{1,17},{... | collective-permute-start | bytes 393224 | tf_op jit(solution)/shard_map/ppermute | solution.py:606
  30.7 1.3 %collective-permute-start.7 = (bf16[128,512]{1,0:T(8,128)(2,1)S(1)}, bf16[128,512]{1,0:T(8,128)(2,1)S(1)}, u32[]{:S(2)}, u32[]{:S(2)}) collective-permute-start(bf16[128,512]{1,0:T(8,128)(2,1)S(1)} %get-tuple-element.20), channel_id=1, source_target_pairs={{0,8},{4,12},{8,0},{12,4},{16,24},{20,28},{24,16},{28,20},{1,9},{5... | collective-permute-start | bytes 393224 | tf_op jit(solution)/shard_map/ppermute | solution.py:606
  31.9 3.5 %collective-permute-done.5.refs_1_ = bf16[128,512]{1,0:T(8,128)(2,1)S(1)} collective-permute-done((bf16[128,512]{1,0:T(8,128)(2,1)S(1)}, bf16[128,512]{1,0:T(8,128)(2,1)S(1)}, u32[]{:S(2)}, u32[]{:S(2)}) %collective-permute-start.5) | collective-permute-done | bytes 131104 | tf_op jit(solution)/shard_map/ppermute | solution.py:606
  35.4 1.0 %collective-permute-done.6.refs_2_ = bf16[128,512]{1,0:T(8,128)(2,1)S(1)} collective-permute-done((bf16[128,512]{1,0:T(8,128)(2,1)S(1)}, bf16[128,512]{1,0:T(8,128)(2,1)S(1)}, u32[]{:S(2)}, u32[]{:S(2)}) %collective-permute-start.6) | collective-permute-done | bytes 131104 | tf_op jit(solution)/shard_map/ppermute | solution.py:606
  36.4 0.1 collective-permute-done.7.refs_3_
  36.5 0.9 %placed_blocks.1 = (bf16[128,1024]{1,0:T(8,128)(2,1)}, bf16[128,1024]{1,0:T(8,128)(2,1)}) custom-call(bf16[128,512]{1,0:T(8,128)(2,1)S(1)} %get-tuple-element.23.refs_0_, bf16[128,512]{1,0:T(8,128)(2,1)S(1)} %collective-permute-done.5.refs_1_, bf16[128,512]{1,0:T(8,128)(2,1)S(1)} %collective-permute-done.6.refs_2_, ...), custom_call_target="tpu_custom_call" | custom-call | tf_op jit(solution)/shard_map/placed_blocks/pallas_call | solution.py:682
  (3 shorter events, 0.1 us)
Async XLA Ops:
  0.6 1.6 %collective-permute-start = (s32[128]{0:T(128)}, s32[128]{0:T(128)S(1)}, u32[]{:S(2)}, u32[]{:S(2)}) collective-permute-start(s32[128]{0:T(128)} %token_ids.1), channel_id=1, source_target_pairs={{0,4},{4,0},{8,12},{12,8},{16,20},{20,16},{24,28},{28,24},{1,5},{5... | collective-permute-start | bytes 1544 | tf_op jit(solution)/shard_map/ppermute | solution.py:606
  2.3 5.6 %collective-permute-start.1 = (s32[2,128]{1,0:T(2,128)S(1)}, s32[2,128]{1,0:T(2,128)S(1)}, u32[]{:S(2)}, u32[]{:S(2)}) collective-permute-start(s32[2,128]{1,0:T(2,128)S(1)} %pad_add_fusion.refs_0_), channel_id=1, source_target_pairs={{0,24},{4,28},{8,16},{12,20},{16,8},{20,12},{24,0},{28,4},{1,25},{... | collective-permute-start | bytes 3080 | tf_op jit(solution)/shard_map/ppermute | solution.py:606
  5.9 3.6 %collective-permute-start.2 = (s32[2,128]{1,0:T(2,128)S(1)}, s32[2,128]{1,0:T(2,128)S(1)}, u32[]{:S(2)}, u32[]{:S(2)}) collective-permute-start(s32[2,128]{1,0:T(2,128)S(1)} %pad_add_fusion.refs_0_), channel_id=1, source_target_pairs={{0,16},{4,20},{8,24},{12,28},{16,0},{20,4},{24,8},{28,12},{1,17},{... | collective-permute-start | bytes 3080 | tf_op jit(solution)/shard_map/ppermute | solution.py:606
  6.4 3.6 %collective-permute-start.3 = (s32[2,128]{1,0:T(2,128)S(1)}, s32[2,128]{1,0:T(2,128)S(1)}, u32[]{:S(2)}, u32[]{:S(2)}) collective-permute-start(s32[2,128]{1,0:T(2,128)S(1)} %pad_add_fusion.refs_0_), channel_id=1, source_target_pairs={{0,8},{4,12},{8,0},{12,4},{16,24},{20,28},{24,16},{28,20},{1,9},{5... | collective-permute-start | bytes 3080 | tf_op jit(solution)/shard_map/ppermute | solution.py:606
  6.5 3.4 %copy-start = (bf16[512,1024]{1,0:T(8,128)(2,1)S(1)}, bf16[512,1024]{1,0:T(8,128)(2,1)}, u32[]{:S(2)}) copy-start(bf16[512,1024]{1,0:T(8,128)(2,1)} %refs_4_.1) | copy-start | bytes 3145732
  6.5 3.4 %copy-start.1 = (f32[7,1024]{1,0:T(8,128)S(1)}, f32[7,1024]{1,0:T(8,128)}, u32[]{:S(2)}) copy-start(f32[7,1024]{1,0:T(8,128)} %refs_5_.1) | copy-start | bytes 86020
  6.5 3.4 %copy-start.4 = (bf16[768,256]{1,0:T(8,128)(2,1)S(1)}, bf16[768,256]{1,0:T(8,128)(2,1)}, u32[]{:S(2)}) copy-start(bf16[768,256]{1,0:T(8,128)(2,1)} %constant.7.clone.refs_8_) | copy-start | bytes 1179652
  6.5 3.4 %copy-start.5 = (bf16[384,256]{1,0:T(8,128)(2,1)S(1)}, bf16[384,256]{1,0:T(8,128)(2,1)}, u32[]{:S(2)}) copy-start(bf16[384,256]{1,0:T(8,128)(2,1)} %constant.8.clone.refs_9_) | copy-start | bytes 589828
  13.4 13.3 %collective-permute-start.4 = (bf16[1024,128]{1,0:T(8,128)(2,1)S(1)}, bf16[1024,128]{1,0:T(8,128)(2,1)S(1)}, u32[]{:S(2)}, u32[]{:S(2)}) collective-permute-start(bf16[1024,128]{1,0:T(8,128)(2,1)S(1)} %get-tuple-element.18.own), channel_id=1, source_target_pairs={{0,4},{4,0},{8,12},{12,8},{16,20},{20,16},{24,28},{28,24},{1,5},{5... | collective-permute-start | bytes 786440 | tf_op jit(solution)/shard_map/ppermute | solution.py:606
  13.5 13.3 %copy-start.2 = (f32[1024]{0:T(1024)S(1)}, f32[1024]{0:T(1024)}, u32[]{:S(2)}) copy-start(f32[1024]{0:T(1024)} %param.17) | copy-start | bytes 12292
  13.5 13.2 %copy-start.3 = (f32[1024]{0:T(1024)S(1)}, f32[1024]{0:T(1024)}, u32[]{:S(2)}) copy-start(f32[1024]{0:T(1024)} %param.18) | copy-start | bytes 12292
  28.4 7.0 %collective-permute-start.5 = (bf16[128,512]{1,0:T(8,128)(2,1)S(1)}, bf16[128,512]{1,0:T(8,128)(2,1)S(1)}, u32[]{:S(2)}, u32[]{:S(2)}) collective-permute-start(bf16[128,512]{1,0:T(8,128)(2,1)S(1)} %get-tuple-element.22), channel_id=1, source_target_pairs={{0,24},{4,28},{8,16},{12,20},{16,8},{20,12},{24,0},{28,4},{1,25},{... | collective-permute-start | bytes 393224 | tf_op jit(solution)/shard_map/ppermute | solution.py:606
  29.2 7.2 %collective-permute-start.6 = (bf16[128,512]{1,0:T(8,128)(2,1)S(1)}, bf16[128,512]{1,0:T(8,128)(2,1)S(1)}, u32[]{:S(2)}, u32[]{:S(2)}) collective-permute-start(bf16[128,512]{1,0:T(8,128)(2,1)S(1)} %get-tuple-element.21), channel_id=1, source_target_pairs={{0,16},{4,20},{8,24},{12,28},{16,0},{20,4},{24,8},{28,12},{1,17},{... | collective-permute-start | bytes 393224 | tf_op jit(solution)/shard_map/ppermute | solution.py:606
  30.7 5.8 %collective-permute-start.7 = (bf16[128,512]{1,0:T(8,128)(2,1)S(1)}, bf16[128,512]{1,0:T(8,128)(2,1)S(1)}, u32[]{:S(2)}, u32[]{:S(2)}) collective-permute-start(bf16[128,512]{1,0:T(8,128)(2,1)S(1)} %get-tuple-element.20), channel_id=1, source_target_pairs={{0,8},{4,12},{8,0},{12,4},{16,24},{20,28},{24,16},{28,20},{1,9},{5... | collective-permute-start | bytes 393224 | tf_op jit(solution)/shard_map/ppermute | solution.py:606
where the time goes:
time: 37.6 us; the launch traced here: 37.4 us
  blocking collectives  13.2 us (35%)
  starting transfers between devices  8.37 us (22%)
  Pallas kernels  8.31 us (22%)
  waiting for transfers between devices  6.65 us (18%)
  between operations  0.74 us (2%)
    all_to_all x1, blocking collectives, by_head(): lax.all_to_all(jnp.broadcast_to(square_sums[None], (devices, seq_count, b...  13.2 us
    ppermute x8, starting transfers between devices, exchange(): lax.ppermute(value, 'seq', [(i, i ^ apart) for i in range(seq_count)])  8.37 us
    ppermute x8, waiting for transfers between devices, exchange(): lax.ppermute(value, 'seq', [(i, i ^ apart) for i in range(seq_count)])  6.65 us
    pallas_call x1, Pallas kernels, by_head(): pl.pallas_call(functools.partial(conv_kernel, piece_count=len(pieces)), o...  3.42 us
    pallas_call x1, Pallas kernels, by_head(): pl.pallas_call(functools.partial(attend_kernel, channel_count=width_dev *...  1.6 us
    pallas_call x1, Pallas kernels, by_head(): pl.pallas_call(response_kernel, out_shape=[jax.ShapeDtypeStruct((2 * bloc...  1.34 us
    pallas_call x1, Pallas kernels, by_head(): pl.pallas_call(fetch_kernel, out_shape=[jax.ShapeDtypeStruct((block,), jn...  1.08 us
    pallas_call x1, Pallas kernels, by_head(): pl.pallas_call(place_kernel, out_shape=[jax.ShapeDtypeStruct((block, widt...  0.87 us
  transfers between devices with their start and end apart: 8, of which 5 were waited for; matrix products, arithmetic and copies ran while one was open for 0% of the time, Pallas kernels for 6%

commit v1 on v0

--- a/solution.py
+++ b/solution.py
@@ -556,14 +556,11 @@
 
     def blend(chip, side, weights, row_total):
         reach = (chip + 1) * 2 * block
-        start = pl.multiple_of((2 * chip + core) * block, block)
         place = lax.bitwise_xor(me // 2, chip)
         half = lax.bitwise_xor(core, side)
         blended = dot32(weights, values[side, 0:reach, :])
         lanes = pl.ds(pl.multiple_of(half * width, width), width)
         out[place, :, lanes] = (blended / row_total).astype(jnp.bfloat16)
-        lanes = pl.ds(pl.multiple_of((2 + half) * width, width), width)
-        out[place, :, lanes] = signals[side][pl.ds(start, block), :]
 
     for b in range(count):
         normalise(b)
@@ -578,14 +575,28 @@
             blend(*chains[turn - 2], *weighed.pop(turn - 2))
 
 
+def outgoing_kernel(own, other, out):
+    width = own.shape[1]
+    block = out.shape[1]
+    me = lax.axis_index("seq")
+    core = lax.rem(me, 2)
+    for i in range(out.shape[0]):
+        start = pl.multiple_of((2 * lax.bitwise_xor(me // 2, i) + core) * block, block)
+        for side, signal in enumerate((own, other)):
+            lanes = pl.ds(pl.multiple_of(lax.bitwise_xor(core, side) * width, width), width)
+            out[i, :, lanes] = signal[pl.ds(start, block), :]
+
+
+def hold_kernel(*refs):
+    refs[-1][...] = refs[0][...]
+
+
 def place_kernel(*refs):
-    blocks, (hyena, attended) = refs[:-2], refs[-2:]
-    span = blocks[0].shape[1] // 2
+    blocks, out = refs[:-1], refs[-1]
+    span = blocks[0].shape[1]
     chip = lax.axis_index("seq") // 2
     for i, block in zip(far_first(len(blocks)), blocks):
-        lanes = pl.ds(pl.multiple_of(lax.bitwise_xor(chip, i) * span, span), span)
-        attended[:, lanes] = block[:, 0:span]
-        hyena[:, lanes] = block[:, span : 2 * span]
+        out[:, pl.ds(pl.multiple_of(lax.bitwise_xor(chip, i) * span, span), span)] = block[...]
 
 
 def by_head(
@@ -668,9 +679,42 @@
     all_sums = lax.all_to_all(
         jnp.broadcast_to(square_sums[None], (devices, seq_count, block)), ("seq", "ch"), 0, 0, tiled=True
     )
+
+    def placed(blocks, name):
+        return pl.pallas_call(
+            place_kernel,
+            out_shape=jax.ShapeDtypeStruct((block, width_dev), bf16),
+            in_specs=[whole] * len(blocks),
+            out_specs=whole,
+            compiler_params=params,
+            cost_estimate=pl.CostEstimate(flops=10**9, bytes_accessed=10**6, transcendentals=0),
+            name=name,
+        )(*blocks)
+
+    def held(value, others):
+        return pl.pallas_call(
+            hold_kernel,
+            out_shape=jax.ShapeDtypeStruct(value.shape, value.dtype),
+            in_specs=[whole] + [pl.BlockSpec(memory_space=pl.ANY)] * len(others),
+            out_specs=whole,
+            compiler_params=params,
+            name="held_block",
+        )(value, *others)
+
+    order = far_first(seq_count // 2)
+    hyena_blocks = pl.pallas_call(
+        outgoing_kernel,
+        out_shape=jax.ShapeDtypeStruct((seq_count // 2, block, 2 * width), bf16),
+        in_specs=[whole, whole],
+        out_specs=whole,
+        compiler_params=params,
+        cost_estimate=pl.CostEstimate(flops=2 * 10**9, bytes_accessed=10**6, transcendentals=0),
+        name="hyena_blocks",
+    )(hyena, other)
+    hyena_parts = [hyena_blocks[0]] + [exchange(hyena_blocks[i], 2 * i) for i in order[1:]]
     outgoing = pl.pallas_call(
         functools.partial(attend_kernel, channel_count=width_dev * ch_count),
-        out_shape=jax.ShapeDtypeStruct((seq_count // 2, block, 4 * width), bf16),
+        out_shape=jax.ShapeDtypeStruct((seq_count // 2, block, 2 * width), bf16),
         in_specs=[whole] * 5,
         out_specs=whole,
         scratch_shapes=[pltpu.VMEM((2, length, width), bf16)] * 3,
@@ -678,15 +722,9 @@
         cost_estimate=pl.CostEstimate(flops=2 * 10**9, bytes_accessed=10**6, transcendentals=10**6),
         name="attention",
     )(hyena, other, all_sums, query_gain.reshape(1, width_dev), key_gain.reshape(1, width_dev))
-    blocks = [outgoing[0]] + [exchange(outgoing[i], 2 * i) for i in far_first(seq_count // 2)[1:]]
-    return pl.pallas_call(
-        place_kernel,
-        out_shape=[jax.ShapeDtypeStruct((block, width_dev), bf16)] * 2,
-        in_specs=[whole] * len(blocks),
-        out_specs=[whole, whole],
-        compiler_params=params,
-        name="placed_blocks",
-    )(*blocks)
+    last = held(outgoing[order[-1]], hyena_parts[1:])
+    parts = [outgoing[0]] + [exchange(outgoing[i], 2 * i) for i in order[1:-1]] + [exchange(last, 2 * order[-1])]
+    return placed(hyena_parts, "placed_hyena"), placed(parts, "placed_attended")
 
 
 def on_device(*operands):

time: 37.6 us -> 36.7 us (0.976)
  blocking collectives: 13.2 us -> 0 us
  starting transfers between devices: 8.37 us -> 17 us
  waiting for transfers between devices: 6.65 us -> 9.08 us
  local copies, waits for them, and re-layouts: 0.07 us -> 0.73 us
  Pallas kernels: 8.31 us -> 8.93 us
    all_to_all x1 -> x0, blocking collectives: 13.2 us -> none  [by_head(): lax.all_to_all(jnp.broadcast_to(square_sums[None], (devices, seq_count, b...]
    all_to_all x0 -> x1, starting transfers between devices: none -> 5.02 us  [by_head(): lax.all_to_all(jnp.broadcast_to(square_sums[None], (devices, seq_count, b...]
    all_to_all x0 -> x1, waiting for transfers between devices: none -> 4.71 us  [by_head(): lax.all_to_all(jnp.broadcast_to(square_sums[None], (devices, seq_count, b...]
    ppermute x8 -> x11, starting transfers between devices: 8.37 us -> 12 us  [exchange(): lax.ppermute(value, 'seq', [(i, i ^ apart) for i in range(seq_count)])]
    ppermute x8 -> x11, waiting for transfers between devices: 6.65 us -> 4.38 us  [exchange(): lax.ppermute(value, 'seq', [(i, i ^ apart) for i in range(seq_count)])]
    pallas_call x1 -> x4, Pallas kernels: 0.87 us -> 1.55 us  [the longest x2 1.47 us: placed(): pl.pallas_call(place_kernel, out_shape=jax.ShapeDtypeStruct((block, width...]
    broadcast_in_dim x1, local copies, waits for them, and re-layouts: 0.01 us -> 0.66 us  [by_head(): jnp.broadcast_to(square_sums[None], (devices, seq_count, block))]
  transfers between devices with their start and end apart: 8 -> 12, of which waited for: 5 -> 6; matrix products, arithmetic and copies ran while one was open for 0% -> 2% of each run, Pallas kernels for 6% -> 13%
where the time goes in v1:
time: 36.7 us; the launch traced here: 36.5 us
  starting transfers between devices  17 us (46%)
  waiting for transfers between devices  9.08 us (25%)
  Pallas kernels  8.93 us (24%)
  between operations  0.77 us (2%)
  local copies, waits for them, and re-layouts  0.73 us (2%)
    ppermute x11, starting transfers between devices, exchange(): lax.ppermute(value, 'seq', [(i, i ^ apart) for i in range(seq_count)])  12 us
    all_to_all x1, starting transfers between devices, by_head(): lax.all_to_all(jnp.broadcast_to(square_sums[None], (devices, seq_count, b...  5.02 us
    all_to_all x1, waiting for transfers between devices, by_head(): lax.all_to_all(jnp.broadcast_to(square_sums[None], (devices, seq_count, b...  4.71 us
    ppermute x11, waiting for transfers between devices, exchange(): lax.ppermute(value, 'seq', [(i, i ^ apart) for i in range(seq_count)])  4.38 us
    pallas_call x1, Pallas kernels, by_head(): pl.pallas_call(functools.partial(conv_kernel, piece_count=len(pieces)), o...  3.39 us
    pallas_call x1, Pallas kernels, by_head(): pl.pallas_call(functools.partial(attend_kernel, channel_count=width_dev *...  1.59 us
    pallas_call x2, Pallas kernels, placed(): pl.pallas_call(place_kernel, out_shape=jax.ShapeDtypeStruct((block, width...  1.47 us
    pallas_call x1, Pallas kernels, by_head(): pl.pallas_call(response_kernel, out_shape=[jax.ShapeDtypeStruct((2 * bloc...  1.33 us
  transfers between devices with their start and end apart: 12, of which 6 were waited for; matrix products, arithmetic and copies ran while one was open for 2% of the time, Pallas kernels for 13%

profile of v1, /device:TPU:0, one launch (start us, length us, event | category | flops | bytes accessed | tf_op | source)
XLA Modules:
  0.0 36.5 jit_solution(7333203345965863549)
XLA Ops:
  0.6 0.5 %collective-permute-start = (s32[128]{0:T(128)}, s32[128]{0:T(128)S(1)}, u32[]{:S(2)}, u32[]{:S(2)}) collective-permute-start(s32[128]{0:T(128)} %token_ids.1), channel_id=1, source_target_pairs={{0,4},{4,0},{8,12},{12,8},{16,20},{20,16},{24,28},{28,24},{1,5},{5... | collective-permute-start | bytes 1544 | tf_op jit(solution)/shard_map/ppermute | solution.py:617
  1.1 1.1 %fetched_operands.1 = (s32[128]{0:T(128)S(1)}, f32[16,128]{1,0:T(8,128)S(1)}, f32[16,128]{1,0:T(8,128)S(1)}, f32[128,128]{1,0:T(8,128)S(1)}, bf16[512,256]{1,0:T(8,128)(2,1)S(1)}) custom-call(s32[128]{0:T(128)} %token_ids.1, f32[16,1024]{1,0:T(8,128)} %residue.1, f32[16,1024]{1,0:T(8,128)} %rate.1, f32[128,1024]{1,0:T(8,128)} %medium.1, ...), custom_call_target="tpu_custom_call" | custom-call | flops 1000000000 | bytes 2000000 | tf_op jit(solution)/shard_map/fetched_operands/pallas_call | solution.py:627
  2.2 0.0 collective-permute-done
  2.3 3.6 %collective-permute-start.1 = (s32[2,128]{1,0:T(2,128)S(1)}, s32[2,128]{1,0:T(2,128)S(1)}, u32[]{:S(2)}, u32[]{:S(2)}) collective-permute-start(s32[2,128]{1,0:T(2,128)S(1)} %pad_add_fusion.refs_0_), channel_id=1, source_target_pairs={{0,24},{4,28},{8,16},{12,20},{16,8},{20,12},{24,0},{28,4},{1,25},{... | collective-permute-start | bytes 3080 | tf_op jit(solution)/shard_map/ppermute | solution.py:617
  5.9 0.5 %collective-permute-start.2 = (s32[2,128]{1,0:T(2,128)S(1)}, s32[2,128]{1,0:T(2,128)S(1)}, u32[]{:S(2)}, u32[]{:S(2)}) collective-permute-start(s32[2,128]{1,0:T(2,128)S(1)} %pad_add_fusion.refs_0_), channel_id=1, source_target_pairs={{0,16},{4,20},{8,24},{12,28},{16,0},{20,4},{24,8},{28,12},{1,17},{... | collective-permute-start | bytes 3080 | tf_op jit(solution)/shard_map/ppermute | solution.py:617
  6.4 0.1 collective-permute-start.3
  6.5 0.0 copy-start
  6.5 0.0 copy-start.1
  6.5 0.0 copy-start.4
  6.5 0.0 copy-start.5
  6.5 1.3 %filter_responses.1 = (f32[256,128]{1,0:T(8,128)S(1)}, f32[256,1024]{1,0:T(8,128)S(1)}) custom-call(f32[16,128]{1,0:T(8,128)S(1)} %get-tuple-element.12.residue, f32[16,128]{1,0:T(8,128)S(1)} %get-tuple-element.13.rate, f32[128,128]{1,0:T(8,128)S(1)} %get-tuple-element.14.medium, bf16[512,256]{1,0:T(8,128)(2,1)S(1)} %get-tuple-element.15.table), custom_call_target="tpu_custom_call" | custom-call | flops 2000000000 | bytes 2000000 | tf_op jit(solution)/shard_map/filter_responses/pallas_call | solution.py:645
  7.8 0.0 collective-permute-done.1.refs_1_
  7.8 1.6 %collective-permute-done.2.refs_2_ = s32[2,128]{1,0:T(2,128)S(1)} collective-permute-done((s32[2,128]{1,0:T(2,128)S(1)}, s32[2,128]{1,0:T(2,128)S(1)}, u32[]{:S(2)}, u32[]{:S(2)}) %collective-permute-start.2) | collective-permute-done | bytes 1056 | tf_op jit(solution)/shard_map/ppermute | solution.py:617
  9.4 0.5 %collective-permute-done.3.refs_3_ = s32[2,128]{1,0:T(2,128)S(1)} collective-permute-done((s32[2,128]{1,0:T(2,128)S(1)}, s32[2,128]{1,0:T(2,128)S(1)}, u32[]{:S(2)}, u32[]{:S(2)}) %collective-permute-start.3) | collective-permute-done | bytes 1056 | tf_op jit(solution)/shard_map/ppermute | solution.py:617
  9.9 0.0 copy-done
  9.9 0.0 copy-done.1
  9.9 0.0 copy-done.4
  9.9 0.0 copy-done.5
  10.0 3.4 %gated_convolutions.1 = (bf16[1024,128]{1,0:T(8,128)(2,1)S(1)}, f32[8,128]{1,0:T(8,128)S(1)}) custom-call(s32[2,128]{1,0:T(2,128)S(1)} %pad_add_fusion.refs_0_, s32[2,128]{1,0:T(2,128)S(1)} %collective-permute-done.1.refs_1_, s32[2,128]{1,0:T(2,128)S(1)} %collective-permute-done.2.refs_2_, s32[2,128]{1,0:T(2,128)S(1)} %collective-permute-done.3.refs_3_, ...), custom_call_target="tpu_custom_call" | custom-call | flops 2000000000 | bytes 2000000 | tf_op jit(solution)/shard_map/gated_convolutions/pallas_call | solution.py:658
  13.3 0.1 collective-permute-start.4
  13.4 0.7 %broadcast_in_dim.2 = f32[32,8,128]{2,1,0:T(8,128)} broadcast(f32[8,128]{1,0:T(8,128)S(1)} %get-tuple-element.19), dimensions={1,2} | broadcast | bytes 135168 | tf_op jit(solution)/shard_map/broadcast_in_dim | solution.py:680
  14.1 5.0 %all-to-all-start = ((f32[32,8,128]{2,1,0:T(8,128)}), f32[32,8,128]{2,1,0:T(8,128)S(1)}, u32[]{:S(2)}, u32[]{:S(2)}) async-start(f32[32,8,128]{2,1,0:T(8,128)} %broadcast_in_dim.2), calls=%async_computation | async-start | bytes 262144 | tf_op jit(solution)/shard_map/all_to_all | solution.py:679
  19.1 0.0 collective-permute-done.4.other
  19.1 0.1 hyena_blocks.1
  19.2 0.0 copy-start.3
  19.2 0.0 copy-start.2
  19.3 2.7 %collective-permute-start.5 = (bf16[128,256]{1,0:T(8,128)(2,1)S(1)}, bf16[128,256]{1,0:T(8,128)(2,1)S(1)}, u32[]{:S(2)}, u32[]{:S(2)}) collective-permute-start(bf16[128,256]{1,0:T(8,128)(2,1)S(1)} %get-tuple-element.26), channel_id=1, source_target_pairs={{0,24},{4,28},{8,16},{12,20},{16,8},{20,12},{24,0},{28,4},{1,25},{... | collective-permute-start | bytes 196616 | tf_op jit(solution)/shard_map/ppermute | solution.py:617
  22.0 0.6 %collective-permute-start.6 = (bf16[128,256]{1,0:T(8,128)(2,1)S(1)}, bf16[128,256]{1,0:T(8,128)(2,1)S(1)}, u32[]{:S(2)}, u32[]{:S(2)}) collective-permute-start(bf16[128,256]{1,0:T(8,128)(2,1)S(1)} %get-tuple-element.25), channel_id=1, source_target_pairs={{0,16},{4,20},{8,24},{12,28},{16,0},{20,4},{24,8},{28,12},{1,17},{... | collective-permute-start | bytes 196616 | tf_op jit(solution)/shard_map/ppermute | solution.py:617
  22.6 0.3 collective-permute-start.7
  22.8 4.7 %all-to-all-done.sums = f32[32,8,128]{2,1,0:T(8,128)S(1)} async-done(((f32[32,8,128]{2,1,0:T(8,128)}), f32[32,8,128]{2,1,0:T(8,128)S(1)}, u32[]{:S(2)}, u32[]{:S(2)}) %all-to-all-start) | async-done | bytes 131104 | tf_op jit(solution)/shard_map/all_to_all | solution.py:679
  27.5 0.0 copy-done.3
  27.5 0.0 copy-done.2
  27.5 1.6 %attention.1 = bf16[4,128,256]{2,1,0:T(8,128)(2,1)S(1)} custom-call(bf16[1024,128]{1,0:T(8,128)(2,1)S(1)} %get-tuple-element.18.own, bf16[1024,128]{1,0:T(8,128)(2,1)S(1)} %collective-permute-done.4.other, f32[32,8,128]{2,1,0:T(8,128)S(1)} %all-to-all-done.sums, f32[1,1024]{1,0:T(1,128)S(1)} %bitcast.21, f32[1,1024]{1,0:T(1,128)S(1)} %bitcast.22), custom_call_target="tpu_custom_call" | custom-call | flops 2000000000 | bytes 1000000 | tf_op jit(solution)/shard_map/attention/pallas_call | solution.py:715
  29.2 0.8 %collective-permute-start.8 = (bf16[128,256]{1,0:T(8,128)(2,1)S(1)}, bf16[128,256]{1,0:T(8,128)(2,1)S(1)}, u32[]{:S(2)}, u32[]{:S(2)}) collective-permute-start(bf16[128,256]{1,0:T(8,128)(2,1)S(1)} %get-tuple-element.22), channel_id=1, source_target_pairs={{0,24},{4,28},{8,16},{12,20},{16,8},{20,12},{24,0},{28,4},{1,25},{... | collective-permute-start | bytes 196616 | tf_op jit(solution)/shard_map/ppermute | solution.py:617
  30.0 1.5 %collective-permute-start.9 = (bf16[128,256]{1,0:T(8,128)(2,1)S(1)}, bf16[128,256]{1,0:T(8,128)(2,1)S(1)}, u32[]{:S(2)}, u32[]{:S(2)}) collective-permute-start(bf16[128,256]{1,0:T(8,128)(2,1)S(1)} %get-tuple-element.21), channel_id=1, source_target_pairs={{0,16},{4,20},{8,24},{12,28},{16,0},{20,4},{24,8},{28,12},{1,17},{... | collective-permute-start | bytes 196616 | tf_op jit(solution)/shard_map/ppermute | solution.py:617
  31.4 0.0 collective-permute-done.5.refs_1_
  31.5 0.0 collective-permute-done.6.refs_2_
  31.5 0.0 collective-permute-done.7.refs_3_
  31.5 1.3 %collective-permute-start.10 = (bf16[128,256]{1,0:T(8,128)(2,1)S(1)}, bf16[128,256]{1,0:T(8,128)(2,1)S(1)}, u32[]{:S(2)}, u32[]{:S(2)}) collective-permute-start(bf16[128,256]{1,0:T(8,128)(2,1)S(1)} %held_block.1), channel_id=1, source_target_pairs={{0,8},{4,12},{8,0},{12,4},{16,24},{20,28},{24,16},{28,20},{1,9},{5... | collective-permute-start | bytes 196616 | tf_op jit(solution)/shard_map/ppermute | solution.py:617
  32.8 0.7 %placed_hyena.1 = bf16[128,1024]{1,0:T(8,128)(2,1)} custom-call(bf16[128,256]{1,0:T(8,128)(2,1)S(1)} %get-tuple-element.27.refs_0_, bf16[128,256]{1,0:T(8,128)(2,1)S(1)} %collective-permute-done.5.refs_1_, bf16[128,256]{1,0:T(8,128)(2,1)S(1)} %collective-permute-done.6.refs_2_, bf16[128,256]{1,0:T(8,128)(2,1)S(1)} %collective-permute-done.7.refs_3_), custom_call_target="tpu_custom_call" | custom-call | flops 1000000000 | bytes 1000000 | tf_op jit(solution)/shard_map/placed_hyena/pallas_call | solution.py:684
  33.5 1.0 %collective-permute-done.8.refs_1_ = bf16[128,256]{1,0:T(8,128)(2,1)S(1)} collective-permute-done((bf16[128,256]{1,0:T(8,128)(2,1)S(1)}, bf16[128,256]{1,0:T(8,128)(2,1)S(1)}, u32[]{:S(2)}, u32[]{:S(2)}) %collective-permute-start.8) | collective-permute-done | bytes 65568 | tf_op jit(solution)/shard_map/ppermute | solution.py:617
  34.5 0.4 %collective-permute-done.9.refs_2_ = bf16[128,256]{1,0:T(8,128)(2,1)S(1)} collective-permute-done((bf16[128,256]{1,0:T(8,128)(2,1)S(1)}, bf16[128,256]{1,0:T(8,128)(2,1)S(1)}, u32[]{:S(2)}, u32[]{:S(2)}) %collective-permute-start.9) | collective-permute-done | bytes 65568 | tf_op jit(solution)/shard_map/ppermute | solution.py:617
  34.9 0.9 %collective-permute-done.10.refs_3_ = bf16[128,256]{1,0:T(8,128)(2,1)S(1)} collective-permute-done((bf16[128,256]{1,0:T(8,128)(2,1)S(1)}, bf16[128,256]{1,0:T(8,128)(2,1)S(1)}, u32[]{:S(2)}, u32[]{:S(2)}) %collective-permute-start.10) | collective-permute-done | bytes 65568 | tf_op jit(solution)/shard_map/ppermute | solution.py:617
  35.8 0.7 %placed_attended.1 = bf16[128,1024]{1,0:T(8,128)(2,1)} custom-call(bf16[128,256]{1,0:T(8,128)(2,1)S(1)} %get-tuple-element.23.refs_0_, bf16[128,256]{1,0:T(8,128)(2,1)S(1)} %collective-permute-done.8.refs_1_, bf16[128,256]{1,0:T(8,128)(2,1)S(1)} %collective-permute-done.9.refs_2_, bf16[128,256]{1,0:T(8,128)(2,1)S(1)} %collective-permute-done.10.refs_3_), custom_call_target="tpu_custom_call" | custom-call | flops 1000000000 | bytes 1000000 | tf_op jit(solution)/shard_map/placed_attended/pallas_call | solution.py:684
  (4 shorter events, 0.1 us)
Async XLA Ops:
  0.6 1.6 %collective-permute-start = (s32[128]{0:T(128)}, s32[128]{0:T(128)S(1)}, u32[]{:S(2)}, u32[]{:S(2)}) collective-permute-start(s32[128]{0:T(128)} %token_ids.1), channel_id=1, source_target_pairs={{0,4},{4,0},{8,12},{12,8},{16,20},{20,16},{24,28},{28,24},{1,5},{5... | collective-permute-start | bytes 1544 | tf_op jit(solution)/shard_map/ppermute | solution.py:617
  2.3 5.6 %collective-permute-start.1 = (s32[2,128]{1,0:T(2,128)S(1)}, s32[2,128]{1,0:T(2,128)S(1)}, u32[]{:S(2)}, u32[]{:S(2)}) collective-permute-start(s32[2,128]{1,0:T(2,128)S(1)} %pad_add_fusion.refs_0_), channel_id=1, source_target_pairs={{0,24},{4,28},{8,16},{12,20},{16,8},{20,12},{24,0},{28,4},{1,25},{... | collective-permute-start | bytes 3080 | tf_op jit(solution)/shard_map/ppermute | solution.py:617
  5.9 3.6 %collective-permute-start.2 = (s32[2,128]{1,0:T(2,128)S(1)}, s32[2,128]{1,0:T(2,128)S(1)}, u32[]{:S(2)}, u32[]{:S(2)}) collective-permute-start(s32[2,128]{1,0:T(2,128)S(1)} %pad_add_fusion.refs_0_), channel_id=1, source_target_pairs={{0,16},{4,20},{8,24},{12,28},{16,0},{20,4},{24,8},{28,12},{1,17},{... | collective-permute-start | bytes 3080 | tf_op jit(solution)/shard_map/ppermute | solution.py:617
  6.4 3.6 %collective-permute-start.3 = (s32[2,128]{1,0:T(2,128)S(1)}, s32[2,128]{1,0:T(2,128)S(1)}, u32[]{:S(2)}, u32[]{:S(2)}) collective-permute-start(s32[2,128]{1,0:T(2,128)S(1)} %pad_add_fusion.refs_0_), channel_id=1, source_target_pairs={{0,8},{4,12},{8,0},{12,4},{16,24},{20,28},{24,16},{28,20},{1,9},{5... | collective-permute-start | bytes 3080 | tf_op jit(solution)/shard_map/ppermute | solution.py:617
  6.5 3.4 %copy-start = (bf16[512,1024]{1,0:T(8,128)(2,1)S(1)}, bf16[512,1024]{1,0:T(8,128)(2,1)}, u32[]{:S(2)}) copy-start(bf16[512,1024]{1,0:T(8,128)(2,1)} %refs_4_.1) | copy-start | bytes 3145732
  6.5 3.4 %copy-start.1 = (f32[7,1024]{1,0:T(8,128)S(1)}, f32[7,1024]{1,0:T(8,128)}, u32[]{:S(2)}) copy-start(f32[7,1024]{1,0:T(8,128)} %refs_5_.1) | copy-start | bytes 86020
  6.5 3.4 %copy-start.4 = (bf16[768,256]{1,0:T(8,128)(2,1)S(1)}, bf16[768,256]{1,0:T(8,128)(2,1)}, u32[]{:S(2)}) copy-start(bf16[768,256]{1,0:T(8,128)(2,1)} %constant.7.clone.refs_8_) | copy-start | bytes 1179652
  6.5 3.4 %copy-start.5 = (bf16[384,256]{1,0:T(8,128)(2,1)S(1)}, bf16[384,256]{1,0:T(8,128)(2,1)}, u32[]{:S(2)}) copy-start(bf16[384,256]{1,0:T(8,128)(2,1)} %constant.8.clone.refs_9_) | copy-start | bytes 589828
  13.3 5.8 %collective-permute-start.4 = (bf16[1024,128]{1,0:T(8,128)(2,1)S(1)}, bf16[1024,128]{1,0:T(8,128)(2,1)S(1)}, u32[]{:S(2)}, u32[]{:S(2)}) collective-permute-start(bf16[1024,128]{1,0:T(8,128)(2,1)S(1)} %get-tuple-element.18.own), channel_id=1, source_target_pairs={{0,4},{4,0},{8,12},{12,8},{16,20},{20,16},{24,28},{28,24},{1,5},{5... | collective-permute-start | bytes 786440 | tf_op jit(solution)/shard_map/ppermute | solution.py:617
  14.1 13.4 %all-to-all-start = ((f32[32,8,128]{2,1,0:T(8,128)}), f32[32,8,128]{2,1,0:T(8,128)S(1)}, u32[]{:S(2)}, u32[]{:S(2)}) async-start(f32[32,8,128]{2,1,0:T(8,128)} %broadcast_in_dim.2), calls=%async_computation | async-start | bytes 262144 | tf_op jit(solution)/shard_map/all_to_all | solution.py:679
  19.2 8.3 %copy-start.3 = (f32[1024]{0:T(1024)S(1)}, f32[1024]{0:T(1024)}, u32[]{:S(2)}) copy-start(f32[1024]{0:T(1024)} %param.18) | copy-start | bytes 12292
  19.2 8.3 %copy-start.2 = (f32[1024]{0:T(1024)S(1)}, f32[1024]{0:T(1024)}, u32[]{:S(2)}) copy-start(f32[1024]{0:T(1024)} %param.17) | copy-start | bytes 12292
  19.3 12.2 %collective-permute-start.5 = (bf16[128,256]{1,0:T(8,128)(2,1)S(1)}, bf16[128,256]{1,0:T(8,128)(2,1)S(1)}, u32[]{:S(2)}, u32[]{:S(2)}) collective-permute-start(bf16[128,256]{1,0:T(8,128)(2,1)S(1)} %get-tuple-element.26), channel_id=1, source_target_pairs={{0,24},{4,28},{8,16},{12,20},{16,8},{20,12},{24,0},{28,4},{1,25},{... | collective-permute-start | bytes 196616 | tf_op jit(solution)/shard_map/ppermute | solution.py:617
  22.0 9.5 %collective-permute-start.6 = (bf16[128,256]{1,0:T(8,128)(2,1)S(1)}, bf16[128,256]{1,0:T(8,128)(2,1)S(1)}, u32[]{:S(2)}, u32[]{:S(2)}) collective-permute-start(bf16[128,256]{1,0:T(8,128)(2,1)S(1)} %get-tuple-element.25), channel_id=1, source_target_pairs={{0,16},{4,20},{8,24},{12,28},{16,0},{20,4},{24,8},{28,12},{1,17},{... | collective-permute-start | bytes 196616 | tf_op jit(solution)/shard_map/ppermute | solution.py:617
  22.6 8.9 %collective-permute-start.7 = (bf16[128,256]{1,0:T(8,128)(2,1)S(1)}, bf16[128,256]{1,0:T(8,128)(2,1)S(1)}, u32[]{:S(2)}, u32[]{:S(2)}) collective-permute-start(bf16[128,256]{1,0:T(8,128)(2,1)S(1)} %get-tuple-element.24), channel_id=1, source_target_pairs={{0,8},{4,12},{8,0},{12,4},{16,24},{20,28},{24,16},{28,20},{1,9},{5... | collective-permute-start | bytes 196616 | tf_op jit(solution)/shard_map/ppermute | solution.py:617
  29.2 5.3 %collective-permute-start.8 = (bf16[128,256]{1,0:T(8,128)(2,1)S(1)}, bf16[128,256]{1,0:T(8,128)(2,1)S(1)}, u32[]{:S(2)}, u32[]{:S(2)}) collective-permute-start(bf16[128,256]{1,0:T(8,128)(2,1)S(1)} %get-tuple-element.22), channel_id=1, source_target_pairs={{0,24},{4,28},{8,16},{12,20},{16,8},{20,12},{24,0},{28,4},{1,25},{... | collective-permute-start | bytes 196616 | tf_op jit(solution)/shard_map/ppermute | solution.py:617
  30.0 5.0 %collective-permute-start.9 = (bf16[128,256]{1,0:T(8,128)(2,1)S(1)}, bf16[128,256]{1,0:T(8,128)(2,1)S(1)}, u32[]{:S(2)}, u32[]{:S(2)}) collective-permute-start(bf16[128,256]{1,0:T(8,128)(2,1)S(1)} %get-tuple-element.21), channel_id=1, source_target_pairs={{0,16},{4,20},{8,24},{12,28},{16,0},{20,4},{24,8},{28,12},{1,17},{... | collective-permute-start | bytes 196616 | tf_op jit(solution)/shard_map/ppermute | solution.py:617
  31.5 4.3 %collective-permute-start.10 = (bf16[128,256]{1,0:T(8,128)(2,1)S(1)}, bf16[128,256]{1,0:T(8,128)(2,1)S(1)}, u32[]{:S(2)}, u32[]{:S(2)}) collective-permute-start(bf16[128,256]{1,0:T(8,128)(2,1)S(1)} %held_block.1), channel_id=1, source_target_pairs={{0,8},{4,12},{8,0},{12,4},{16,24},{20,28},{24,16},{28,20},{1,9},{5... | collective-permute-start | bytes 196616 | tf_op jit(solution)/shard_map/ppermute | solution.py:617

commit v2 on v1

--- a/solution.py
+++ b/solution.py
@@ -295,6 +295,9 @@
     forward, backward = parts(forward), parts(backward)
     first, second, third = np.split(forward[:, :block], 3)
     taps = np.concatenate([np.concatenate([first, second], axis=1), np.concatenate([first, third], axis=1)], axis=0)
+    forward = np.concatenate(np.split(forward, 3), axis=1)
+    first, second, third = np.split(backward, 3)
+    backward = np.concatenate([first, second, first, third, second, first], axis=1)
     return forward, backward, taps
 
 
@@ -321,10 +324,6 @@
 
 def dot32(left, right):
     return jnp.dot(left, right, preferred_element_type=jnp.float32)
-
-
-def far_first(count):
-    return [0, *range(count - 1, 0, -1)]
 
 
 def own_lanes(width):
@@ -387,15 +386,15 @@
 def conv_kernel(*refs, piece_count):
     pieces = refs[:piece_count]
     (embedding, short, medium_resp, long_resp, forward, backward, hyena, sums) = refs[piece_count : piece_count + 8]
-    ids, ordered, padded, row_sums = refs[piece_count + 8 :]
+    ids, ordered, padded, row_sums, copied_sums, sem = refs[piece_count + 8 :]
     width = padded.shape[1]
     block = width
     size = 2 * block
     length = hyena.shape[0]
     count = length // block
-    pair = count // 2
+    pair = count
     me = lax.axis_index("seq")
-    for i, piece in zip(far_first(piece_count), pieces):
+    for i, piece in enumerate(pieces):
         ids[2 * i : 2 * i + 2, :] = piece[...]
     for b in range(count):
         ordered[b : b + 1, :] = ids[pl.ds(lax.bitwise_xor(me, b), 1), :]
@@ -431,41 +430,42 @@
             + [jnp.concatenate([gated[turn][b] for b in span], axis=1)],
             axis=0,
         )
-        spectrum = (
-            dot32(forward[0:size, :], signal)
-            + dot32(forward[size : 2 * size, :], signal)
-            + dot32(forward[2 * size : 3 * size, :], signal)
-        )
+        spectrum = dot32(forward[...], jnp.concatenate([signal] * 3, axis=0))
         for i, b in enumerate(span):
             spectra[turn][b] = spectrum[:, i * width : (i + 1) * width]
 
     def multiply(turn, response, chunk):
-        columns = []
-        for b in range(chunk * pair, (chunk + 1) * pair):
-            tiles = [[], []]
-            for first in range(0, block, rows):
-                upper = slice(first, first + rows)
-                lower = slice(block + first, block + first + rows)
-                total_real, total_imag = 0.0, 0.0
-                for part in range(b + 1 if turn else 1):
-                    taps = slice(part * width, (part + 1) * width)
-                    real, imag = spectra[turn][b - part][upper], spectra[turn][b - part][lower]
-                    filt_real, filt_imag = response[upper, taps], response[lower, taps]
-                    total_real = total_real + (real * filt_real - imag * filt_imag)
-                    total_imag = total_imag + (real * filt_imag + imag * filt_real)
-                tiles[0].append(split_three(total_real))
-                tiles[1].append(split_three(total_imag))
-            columns.append([jnp.concatenate([tile[i] for tile in tiles[0] + tiles[1]], axis=0) for i in range(3)])
+        span = range(chunk * pair, (chunk + 1) * pair)
+        sources = range(span[-1] + 1) if turn else span
+        tiles = {b: ([], []) for b in span}
+        for first in range(0, block, rows):
+            sums = {b: ([], []) for b in span}
+            for upper in [slice(i, i + 8) for i in range(first, first + rows, 8)]:
+                lower = slice(block + upper.start, block + upper.stop)
+                data = {b: (spectra[turn][b][upper], spectra[turn][b][lower]) for b in sources}
+                filt = [
+                    (response[upper, i * width : (i + 1) * width], response[lower, i * width : (i + 1) * width])
+                    for i in range(span[-1] + 1 if turn else 1)
+                ]
+                for b in span:
+                    total_real, total_imag = 0.0, 0.0
+                    for part in range(b + 1 if turn else 1):
+                        (real, imag), (filt_real, filt_imag) = data[b - part], filt[part]
+                        total_real = total_real + (real * filt_real - imag * filt_imag)
+                        total_imag = total_imag + (real * filt_imag + imag * filt_real)
+                    sums[b][0].append(total_real)
+                    sums[b][1].append(total_imag)
+            for b in span:
+                for side in range(2):
+                    tiles[b][side].append(split_three(jnp.concatenate(sums[b][side], axis=0)))
+        columns = [
+            [jnp.concatenate([tile[i] for tile in tiles[b][0] + tiles[b][1]], axis=0) for i in range(3)] for b in span
+        ]
         products[turn][chunk] = [jnp.concatenate([column[i] for column in columns], axis=1) for i in range(3)]
 
     def synthesise(turn, chunk):
         up, middle, low = products[turn].pop(chunk)
-        first, second, third = [backward[i * block : (i + 1) * block, :] for i in range(3)]
-        return (
-            dot32(first, up)
-            + (dot32(second, up) + dot32(first, middle))
-            + (dot32(third, up) + dot32(second, middle) + dot32(first, low))
-        )
+        return dot32(backward[...], jnp.concatenate([up, up, middle, up, middle, low], axis=0))
 
     def gate(turn, chunk):
         out = synthesise(turn, chunk)
@@ -507,7 +507,10 @@
         for stage in range(len(stages)):
             if 0 <= turn - stage < chunks:
                 stages[stage](turn - stage)
-    sums[...] = row_sums[...]
+    copied_sums[...] = jnp.broadcast_to(row_sums[...][None], copied_sums.shape)
+    copy = pltpu.make_async_copy(copied_sums, sums, sem)
+    copy.start()
+    copy.wait()
 
 
 def attend_kernel(own, other, sums, query_gain, key_gain, out, queries, keys, values, *, channel_count):
@@ -591,11 +594,11 @@
     refs[-1][...] = refs[0][...]
 
 
-def place_kernel(*refs):
+def place_kernel(*refs, order):
     blocks, out = refs[:-1], refs[-1]
     span = blocks[0].shape[1]
     chip = lax.axis_index("seq") // 2
-    for i, block in zip(far_first(len(blocks)), blocks):
+    for i, block in zip(order, blocks):
         out[:, pl.ds(pl.multiple_of(lax.bitwise_xor(chip, i) * span, span), span)] = block[...]
 
 
@@ -641,7 +644,7 @@
         name="fetched_operands",
     )(*[fetched(value) for value in operands])
     chip_ids = jnp.stack([own_ids, partner_ids])
-    pieces = [chip_ids] + [exchange(chip_ids, 2 * i) for i in far_first(seq_count // 2)[1:]]
+    pieces = [chip_ids] + [exchange(chip_ids, 2 * i) for i in range(1, seq_count // 2)]
     medium_resp, long_resp = pl.pallas_call(
         response_kernel,
         out_shape=[
@@ -655,19 +658,22 @@
         name="filter_responses",
     )(*filters)
 
+    devices = seq_count * ch_count
     hyena, square_sums = pl.pallas_call(
         functools.partial(conv_kernel, piece_count=len(pieces)),
         out_shape=[
             jax.ShapeDtypeStruct((length, width), bf16),
-            jax.ShapeDtypeStruct((seq_count, block), f32),
+            pltpu.HBM((devices, seq_count, block), f32),
         ],
         in_specs=[whole] * (len(pieces) + 6),
-        out_specs=[whole, whole],
+        out_specs=[whole, in_hbm],
         scratch_shapes=[
             pltpu.VMEM((seq_count, block), jnp.int32),
             pltpu.VMEM((seq_count, block), jnp.int32),
             pltpu.VMEM((8 + length, width), f32),
             pltpu.VMEM((seq_count, block), f32),
+            pltpu.VMEM((devices, seq_count, block), f32),
+            pltpu.SemaphoreType.DMA,
         ],
         compiler_params=params,
         cost_estimate=pl.CostEstimate(flops=2 * 10**9, bytes_accessed=2 * 10**6, transcendentals=0),
@@ -675,14 +681,11 @@
     )(*pieces, embedding, short_filter, medium_resp, long_resp, forward, backward)
 
     other = exchange(hyena, 1)
-    devices = seq_count * ch_count
-    all_sums = lax.all_to_all(
-        jnp.broadcast_to(square_sums[None], (devices, seq_count, block)), ("seq", "ch"), 0, 0, tiled=True
-    )
-
-    def placed(blocks, name):
+    all_sums = lax.all_to_all(square_sums, ("seq", "ch"), 0, 0, tiled=True)
+
+    def placed(blocks, name, order):
         return pl.pallas_call(
-            place_kernel,
+            functools.partial(place_kernel, order=(0, *order)),
             out_shape=jax.ShapeDtypeStruct((block, width_dev), bf16),
             in_specs=[whole] * len(blocks),
             out_specs=whole,
@@ -701,7 +704,7 @@
             name="held_block",
         )(value, *others)
 
-    order = far_first(seq_count // 2)
+    order = list(range(1, seq_count // 2))
     hyena_blocks = pl.pallas_call(
         outgoing_kernel,
         out_shape=jax.ShapeDtypeStruct((seq_count // 2, block, 2 * width), bf16),
@@ -711,7 +714,7 @@
         cost_estimate=pl.CostEstimate(flops=2 * 10**9, bytes_accessed=10**6, transcendentals=0),
         name="hyena_blocks",
     )(hyena, other)
-    hyena_parts = [hyena_blocks[0]] + [exchange(hyena_blocks[i], 2 * i) for i in order[1:]]
+    hyena_parts = [hyena_blocks[0]] + [exchange(hyena_blocks[i], 2 * i) for i in order]
     outgoing = pl.pallas_call(
         functools.partial(attend_kernel, channel_count=width_dev * ch_count),
         out_shape=jax.ShapeDtypeStruct((seq_count // 2, block, 2 * width), bf16),
@@ -722,9 +725,9 @@
         cost_estimate=pl.CostEstimate(flops=2 * 10**9, bytes_accessed=10**6, transcendentals=10**6),
         name="attention",
     )(hyena, other, all_sums, query_gain.reshape(1, width_dev), key_gain.reshape(1, width_dev))
-    last = held(outgoing[order[-1]], hyena_parts[1:])
-    parts = [outgoing[0]] + [exchange(outgoing[i], 2 * i) for i in order[1:-1]] + [exchange(last, 2 * order[-1])]
-    return placed(hyena_parts, "placed_hyena"), placed(parts, "placed_attended")
+    last = held(outgoing[order[0]], hyena_parts[1:])
+    parts = [outgoing[0]] + [exchange(outgoing[i], 2 * i) for i in order[:0:-1]] + [exchange(last, 2 * order[0])]
+    return placed(hyena_parts, "placed_hyena", order), placed(parts, "placed_attended", order[::-1])
 
 
 def on_device(*operands):

time: 36.7 us -> 36.5 us (level)
  local copies, waits for them, and re-layouts: 0.73 us -> 0.07 us
  Pallas kernels: 8.93 us -> 9.36 us
    broadcast_in_dim x1 -> x0, local copies, waits for them, and re-layouts: 0.66 us -> none  [by_head(): jnp.broadcast_to(square_sums[None], (devices, seq_count, block))]
    pallas_call x1, Pallas kernels: 3.39 us -> 3.81 us  [by_head(): pl.pallas_call(functools.partial(conv_kernel, piece_count=len(pieces)), o...]
  transfers between devices with their start and end apart: 12 -> 12, of which waited for: 6 -> 6; matrix products, arithmetic and copies ran while one was open for 2% -> 0% of each run, Pallas kernels for 13% -> 13%
where the time goes in v2:
time: 36.5 us; the launch traced here: 36.3 us
  starting transfers between devices  17 us (47%)
  Pallas kernels  9.36 us (26%)
  waiting for transfers between devices  9.07 us (25%)
  between operations  0.78 us (2%)
    ppermute x11, starting transfers between devices, exchange(): lax.ppermute(value, 'seq', [(i, i ^ apart) for i in range(seq_count)])  12 us
    all_to_all x1, starting transfers between devices, by_head(): all_sums = lax.all_to_all(square_sums, ('seq', 'ch'), 0, 0, tiled=True)  5.02 us
    all_to_all x1, waiting for transfers between devices, by_head(): all_sums = lax.all_to_all(square_sums, ('seq', 'ch'), 0, 0, tiled=True)  4.71 us
    ppermute x11, waiting for transfers between devices, exchange(): lax.ppermute(value, 'seq', [(i, i ^ apart) for i in range(seq_count)])  4.36 us
    pallas_call x1, Pallas kernels, by_head(): pl.pallas_call(functools.partial(conv_kernel, piece_count=len(pieces)), o...  3.81 us
    pallas_call x1, Pallas kernels, by_head(): pl.pallas_call(functools.partial(attend_kernel, channel_count=width_dev *...  1.59 us
    pallas_call x2, Pallas kernels, placed(): pl.pallas_call(functools.partial(place_kernel, order=(0, *order)), out_sh...  1.47 us
    pallas_call x1, Pallas kernels, by_head(): pl.pallas_call(response_kernel, out_shape=[jax.ShapeDtypeStruct((2 * bloc...  1.34 us
  transfers between devices with their start and end apart: 12, of which 6 were waited for; matrix products, arithmetic and copies ran while one was open for 0% of the time, Pallas kernels for 13%

profile of v2, /device:TPU:0, one launch (start us, length us, event | category | flops | bytes accessed | tf_op | source)
XLA Modules:
  0.0 36.3 jit_solution(17770793260890390247)
XLA Ops:
  0.6 0.5 %collective-permute-start = (s32[128]{0:T(128)}, s32[128]{0:T(128)S(1)}, u32[]{:S(2)}, u32[]{:S(2)}) collective-permute-start(s32[128]{0:T(128)} %token_ids.1), channel_id=1, source_target_pairs={{0,4},{4,0},{8,12},{12,8},{16,20},{20,16},{24,28},{28,24},{1,5},{5... | collective-permute-start | bytes 1544 | tf_op jit(solution)/shard_map/ppermute | solution.py:620
  1.1 1.1 %fetched_operands.1 = (s32[128]{0:T(128)S(1)}, f32[16,128]{1,0:T(8,128)S(1)}, f32[16,128]{1,0:T(8,128)S(1)}, f32[128,128]{1,0:T(8,128)S(1)}, bf16[512,256]{1,0:T(8,128)(2,1)S(1)}) custom-call(s32[128]{0:T(128)} %token_ids.1, f32[16,1024]{1,0:T(8,128)} %residue.1, f32[16,1024]{1,0:T(8,128)} %rate.1, f32[128,1024]{1,0:T(8,128)} %medium.1, ...), custom_call_target="tpu_custom_call" | custom-call | flops 1000000000 | bytes 2000000 | tf_op jit(solution)/shard_map/fetched_operands/pallas_call | solution.py:630
  2.2 0.0 collective-permute-done
  2.3 3.6 %collective-permute-start.3 = (s32[2,128]{1,0:T(2,128)S(1)}, s32[2,128]{1,0:T(2,128)S(1)}, u32[]{:S(2)}, u32[]{:S(2)}) collective-permute-start(s32[2,128]{1,0:T(2,128)S(1)} %pad_add_fusion.refs_0_), channel_id=1, source_target_pairs={{0,24},{4,28},{8,16},{12,20},{16,8},{20,12},{24,0},{28,4},{1,25},{... | collective-permute-start | bytes 3080 | tf_op jit(solution)/shard_map/ppermute | solution.py:620
  5.9 0.5 %collective-permute-start.2 = (s32[2,128]{1,0:T(2,128)S(1)}, s32[2,128]{1,0:T(2,128)S(1)}, u32[]{:S(2)}, u32[]{:S(2)}) collective-permute-start(s32[2,128]{1,0:T(2,128)S(1)} %pad_add_fusion.refs_0_), channel_id=1, source_target_pairs={{0,16},{4,20},{8,24},{12,28},{16,0},{20,4},{24,8},{28,12},{1,17},{... | collective-permute-start | bytes 3080 | tf_op jit(solution)/shard_map/ppermute | solution.py:620
  6.4 0.1 collective-permute-start.1
  6.5 0.0 copy-start
  6.5 0.0 copy-start.1
  6.5 0.0 copy-start.4
  6.5 0.0 copy-start.5
  6.5 1.3 %filter_responses.1 = (f32[256,128]{1,0:T(8,128)S(1)}, f32[256,1024]{1,0:T(8,128)S(1)}) custom-call(f32[16,128]{1,0:T(8,128)S(1)} %get-tuple-element.12.residue, f32[16,128]{1,0:T(8,128)S(1)} %get-tuple-element.13.rate, f32[128,128]{1,0:T(8,128)S(1)} %get-tuple-element.14.medium, bf16[512,256]{1,0:T(8,128)(2,1)S(1)} %get-tuple-element.15.table), custom_call_target="tpu_custom_call" | custom-call | flops 2000000000 | bytes 2000000 | tf_op jit(solution)/shard_map/filter_responses/pallas_call | solution.py:648
  7.8 0.0 collective-permute-done.3.refs_3_
  7.9 1.6 %collective-permute-done.2.refs_2_ = s32[2,128]{1,0:T(2,128)S(1)} collective-permute-done((s32[2,128]{1,0:T(2,128)S(1)}, s32[2,128]{1,0:T(2,128)S(1)}, u32[]{:S(2)}, u32[]{:S(2)}) %collective-permute-start.2) | collective-permute-done | bytes 1056 | tf_op jit(solution)/shard_map/ppermute | solution.py:620
  9.4 0.5 %collective-permute-done.1.refs_1_ = s32[2,128]{1,0:T(2,128)S(1)} collective-permute-done((s32[2,128]{1,0:T(2,128)S(1)}, s32[2,128]{1,0:T(2,128)S(1)}, u32[]{:S(2)}, u32[]{:S(2)}) %collective-permute-start.1) | collective-permute-done | bytes 1056 | tf_op jit(solution)/shard_map/ppermute | solution.py:620
  9.9 0.0 copy-done
  9.9 0.0 copy-done.1
  9.9 0.0 copy-done.4
  9.9 0.0 copy-done.5
  10.0 3.8 %gated_convolutions.1 = (bf16[1024,128]{1,0:T(8,128)(2,1)S(1)}, f32[32,8,128]{2,1,0:T(8,128)}) custom-call(s32[2,128]{1,0:T(2,128)S(1)} %pad_add_fusion.refs_0_, s32[2,128]{1,0:T(2,128)S(1)} %collective-permute-done.1.refs_1_, s32[2,128]{1,0:T(2,128)S(1)} %collective-permute-done.2.refs_2_, s32[2,128]{1,0:T(2,128)S(1)} %collective-permute-done.3.refs_3_, ...), custom_call_target="tpu_custom_call" | custom-call | flops 2000000000 | bytes 2000000 | tf_op jit(solution)/shard_map/gated_convolutions/pallas_call | solution.py:662
  13.8 0.1 collective-permute-start.4
  13.8 5.0 %all-to-all-start = ((f32[32,8,128]{2,1,0:T(8,128)}), f32[32,8,128]{2,1,0:T(8,128)S(1)}, u32[]{:S(2)}, u32[]{:S(2)}) async-start(f32[32,8,128]{2,1,0:T(8,128)} %get-tuple-element.19), calls=%async_computation | async-start | bytes 262144 | tf_op jit(solution)/shard_map/all_to_all | solution.py:684
  18.9 0.0 collective-permute-done.4.other
  18.9 0.1 hyena_blocks.1
  19.0 0.0 copy-start.3
  19.0 0.0 copy-start.2
  19.0 2.7 %collective-permute-start.7 = (bf16[128,256]{1,0:T(8,128)(2,1)S(1)}, bf16[128,256]{1,0:T(8,128)(2,1)S(1)}, u32[]{:S(2)}, u32[]{:S(2)}) collective-permute-start(bf16[128,256]{1,0:T(8,128)(2,1)S(1)} %get-tuple-element.24), channel_id=1, source_target_pairs={{0,24},{4,28},{8,16},{12,20},{16,8},{20,12},{24,0},{28,4},{1,25},{... | collective-permute-start | bytes 196616 | tf_op jit(solution)/shard_map/ppermute | solution.py:620
  21.7 0.6 %collective-permute-start.6 = (bf16[128,256]{1,0:T(8,128)(2,1)S(1)}, bf16[128,256]{1,0:T(8,128)(2,1)S(1)}, u32[]{:S(2)}, u32[]{:S(2)}) collective-permute-start(bf16[128,256]{1,0:T(8,128)(2,1)S(1)} %get-tuple-element.25), channel_id=1, source_target_pairs={{0,16},{4,20},{8,24},{12,28},{16,0},{20,4},{24,8},{28,12},{1,17},{... | collective-permute-start | bytes 196616 | tf_op jit(solution)/shard_map/ppermute | solution.py:620
  22.3 0.3 collective-permute-start.5
  22.6 4.7 %all-to-all-done.sums = f32[32,8,128]{2,1,0:T(8,128)S(1)} async-done(((f32[32,8,128]{2,1,0:T(8,128)}), f32[32,8,128]{2,1,0:T(8,128)S(1)}, u32[]{:S(2)}, u32[]{:S(2)}) %all-to-all-start) | async-done | bytes 131104 | tf_op jit(solution)/shard_map/all_to_all | solution.py:684
  27.3 0.0 copy-done.3
  27.3 0.0 copy-done.2
  27.3 1.6 %attention.1 = bf16[4,128,256]{2,1,0:T(8,128)(2,1)S(1)} custom-call(bf16[1024,128]{1,0:T(8,128)(2,1)S(1)} %get-tuple-element.18.own, bf16[1024,128]{1,0:T(8,128)(2,1)S(1)} %collective-permute-done.4.other, f32[32,8,128]{2,1,0:T(8,128)S(1)} %all-to-all-done.sums, f32[1,1024]{1,0:T(1,128)S(1)} %bitcast.21, f32[1,1024]{1,0:T(1,128)S(1)} %bitcast.22), custom_call_target="tpu_custom_call" | custom-call | flops 2000000000 | bytes 1000000 | tf_op jit(solution)/shard_map/attention/pallas_call | solution.py:718
  28.9 0.8 %collective-permute-start.9 = (bf16[128,256]{1,0:T(8,128)(2,1)S(1)}, bf16[128,256]{1,0:T(8,128)(2,1)S(1)}, u32[]{:S(2)}, u32[]{:S(2)}) collective-permute-start(bf16[128,256]{1,0:T(8,128)(2,1)S(1)} %get-tuple-element.21), channel_id=1, source_target_pairs={{0,16},{4,20},{8,24},{12,28},{16,0},{20,4},{24,8},{28,12},{1,17},{... | collective-permute-start | bytes 196616 | tf_op jit(solution)/shard_map/ppermute | solution.py:620
  29.8 1.4 %collective-permute-start.8 = (bf16[128,256]{1,0:T(8,128)(2,1)S(1)}, bf16[128,256]{1,0:T(8,128)(2,1)S(1)}, u32[]{:S(2)}, u32[]{:S(2)}) collective-permute-start(bf16[128,256]{1,0:T(8,128)(2,1)S(1)} %get-tuple-element.22), channel_id=1, source_target_pairs={{0,24},{4,28},{8,16},{12,20},{16,8},{20,12},{24,0},{28,4},{1,25},{... | collective-permute-start | bytes 196616 | tf_op jit(solution)/shard_map/ppermute | solution.py:620
  31.2 0.0 collective-permute-done.7.refs_3_
  31.2 0.0 collective-permute-done.6.refs_2_
  31.2 0.0 collective-permute-done.5.refs_1_
  31.2 1.3 %collective-permute-start.10 = (bf16[128,256]{1,0:T(8,128)(2,1)S(1)}, bf16[128,256]{1,0:T(8,128)(2,1)S(1)}, u32[]{:S(2)}, u32[]{:S(2)}) collective-permute-start(bf16[128,256]{1,0:T(8,128)(2,1)S(1)} %held_block.1), channel_id=1, source_target_pairs={{0,8},{4,12},{8,0},{12,4},{16,24},{20,28},{24,16},{28,20},{1,9},{5... | collective-permute-start | bytes 196616 | tf_op jit(solution)/shard_map/ppermute | solution.py:620
  32.6 0.7 %placed_hyena.1 = bf16[128,1024]{1,0:T(8,128)(2,1)} custom-call(bf16[128,256]{1,0:T(8,128)(2,1)S(1)} %get-tuple-element.27.refs_0_, bf16[128,256]{1,0:T(8,128)(2,1)S(1)} %collective-permute-done.5.refs_1_, bf16[128,256]{1,0:T(8,128)(2,1)S(1)} %collective-permute-done.6.refs_2_, bf16[128,256]{1,0:T(8,128)(2,1)S(1)} %collective-permute-done.7.refs_3_), custom_call_target="tpu_custom_call" | custom-call | flops 1000000000 | bytes 1000000 | tf_op jit(solution)/shard_map/placed_hyena/pallas_call | solution.py:687
  33.3 0.6 %collective-permute-done.9.refs_2_ = bf16[128,256]{1,0:T(8,128)(2,1)S(1)} collective-permute-done((bf16[128,256]{1,0:T(8,128)(2,1)S(1)}, bf16[128,256]{1,0:T(8,128)(2,1)S(1)}, u32[]{:S(2)}, u32[]{:S(2)}) %collective-permute-start.9) | collective-permute-done | bytes 65568 | tf_op jit(solution)/shard_map/ppermute | solution.py:620
  33.9 1.0 %collective-permute-done.8.refs_1_ = bf16[128,256]{1,0:T(8,128)(2,1)S(1)} collective-permute-done((bf16[128,256]{1,0:T(8,128)(2,1)S(1)}, bf16[128,256]{1,0:T(8,128)(2,1)S(1)}, u32[]{:S(2)}, u32[]{:S(2)}) %collective-permute-start.8) | collective-permute-done | bytes 65568 | tf_op jit(solution)/shard_map/ppermute | solution.py:620
  34.9 0.6 %collective-permute-done.10.refs_3_ = bf16[128,256]{1,0:T(8,128)(2,1)S(1)} collective-permute-done((bf16[128,256]{1,0:T(8,128)(2,1)S(1)}, bf16[128,256]{1,0:T(8,128)(2,1)S(1)}, u32[]{:S(2)}, u32[]{:S(2)}) %collective-permute-start.10) | collective-permute-done | bytes 65568 | tf_op jit(solution)/shard_map/ppermute | solution.py:620
  35.6 0.7 %placed_attended.1 = bf16[128,1024]{1,0:T(8,128)(2,1)} custom-call(bf16[128,256]{1,0:T(8,128)(2,1)S(1)} %get-tuple-element.23.refs_0_, bf16[128,256]{1,0:T(8,128)(2,1)S(1)} %collective-permute-done.8.refs_1_, bf16[128,256]{1,0:T(8,128)(2,1)S(1)} %collective-permute-done.9.refs_2_, bf16[128,256]{1,0:T(8,128)(2,1)S(1)} %collective-permute-done.10.refs_3_), custom_call_target="tpu_custom_call" | custom-call | flops 1000000000 | bytes 1000000 | tf_op jit(solution)/shard_map/placed_attended/pallas_call | solution.py:687
  (4 shorter events, 0.1 us)
Async XLA Ops:
  0.6 1.6 %collective-permute-start = (s32[128]{0:T(128)}, s32[128]{0:T(128)S(1)}, u32[]{:S(2)}, u32[]{:S(2)}) collective-permute-start(s32[128]{0:T(128)} %token_ids.1), channel_id=1, source_target_pairs={{0,4},{4,0},{8,12},{12,8},{16,20},{20,16},{24,28},{28,24},{1,5},{5... | collective-permute-start | bytes 1544 | tf_op jit(solution)/shard_map/ppermute | solution.py:620
  2.3 5.6 %collective-permute-start.3 = (s32[2,128]{1,0:T(2,128)S(1)}, s32[2,128]{1,0:T(2,128)S(1)}, u32[]{:S(2)}, u32[]{:S(2)}) collective-permute-start(s32[2,128]{1,0:T(2,128)S(1)} %pad_add_fusion.refs_0_), channel_id=1, source_target_pairs={{0,24},{4,28},{8,16},{12,20},{16,8},{20,12},{24,0},{28,4},{1,25},{... | collective-permute-start | bytes 3080 | tf_op jit(solution)/shard_map/ppermute | solution.py:620
  5.9 3.6 %collective-permute-start.2 = (s32[2,128]{1,0:T(2,128)S(1)}, s32[2,128]{1,0:T(2,128)S(1)}, u32[]{:S(2)}, u32[]{:S(2)}) collective-permute-start(s32[2,128]{1,0:T(2,128)S(1)} %pad_add_fusion.refs_0_), channel_id=1, source_target_pairs={{0,16},{4,20},{8,24},{12,28},{16,0},{20,4},{24,8},{28,12},{1,17},{... | collective-permute-start | bytes 3080 | tf_op jit(solution)/shard_map/ppermute | solution.py:620
  6.4 3.6 %collective-permute-start.1 = (s32[2,128]{1,0:T(2,128)S(1)}, s32[2,128]{1,0:T(2,128)S(1)}, u32[]{:S(2)}, u32[]{:S(2)}) collective-permute-start(s32[2,128]{1,0:T(2,128)S(1)} %pad_add_fusion.refs_0_), channel_id=1, source_target_pairs={{0,8},{4,12},{8,0},{12,4},{16,24},{20,28},{24,16},{28,20},{1,9},{5... | collective-permute-start | bytes 3080 | tf_op jit(solution)/shard_map/ppermute | solution.py:620
  6.5 3.4 %copy-start = (bf16[512,1024]{1,0:T(8,128)(2,1)S(1)}, bf16[512,1024]{1,0:T(8,128)(2,1)}, u32[]{:S(2)}) copy-start(bf16[512,1024]{1,0:T(8,128)(2,1)} %refs_4_.1) | copy-start | bytes 3145732
  6.5 3.4 %copy-start.1 = (f32[7,1024]{1,0:T(8,128)S(1)}, f32[7,1024]{1,0:T(8,128)}, u32[]{:S(2)}) copy-start(f32[7,1024]{1,0:T(8,128)} %refs_5_.1) | copy-start | bytes 86020
  6.5 3.4 %copy-start.4 = (bf16[128,1536]{1,0:T(8,128)(2,1)S(1)}, bf16[128,1536]{1,0:T(8,128)(2,1)}, u32[]{:S(2)}) copy-start(bf16[128,1536]{1,0:T(8,128)(2,1)} %constant.8.clone.refs_9_) | copy-start | bytes 1179652
  6.5 3.4 %copy-start.5 = (bf16[256,768]{1,0:T(8,128)(2,1)S(1)}, bf16[256,768]{1,0:T(8,128)(2,1)}, u32[]{:S(2)}) copy-start(bf16[256,768]{1,0:T(8,128)(2,1)} %constant.7.clone.refs_8_) | copy-start | bytes 1179652
  13.8 5.1 %collective-permute-start.4 = (bf16[1024,128]{1,0:T(8,128)(2,1)S(1)}, bf16[1024,128]{1,0:T(8,128)(2,1)S(1)}, u32[]{:S(2)}, u32[]{:S(2)}) collective-permute-start(bf16[1024,128]{1,0:T(8,128)(2,1)S(1)} %get-tuple-element.18.own), channel_id=1, source_target_pairs={{0,4},{4,0},{8,12},{12,8},{16,20},{20,16},{24,28},{28,24},{1,5},{5... | collective-permute-start | bytes 786440 | tf_op jit(solution)/shard_map/ppermute | solution.py:620
  13.8 13.4 %all-to-all-start = ((f32[32,8,128]{2,1,0:T(8,128)}), f32[32,8,128]{2,1,0:T(8,128)S(1)}, u32[]{:S(2)}, u32[]{:S(2)}) async-start(f32[32,8,128]{2,1,0:T(8,128)} %get-tuple-element.19), calls=%async_computation | async-start | bytes 262144 | tf_op jit(solution)/shard_map/all_to_all | solution.py:684
  19.0 8.3 %copy-start.3 = (f32[1024]{0:T(1024)S(1)}, f32[1024]{0:T(1024)}, u32[]{:S(2)}) copy-start(f32[1024]{0:T(1024)} %param.18) | copy-start | bytes 12292
  19.0 8.3 %copy-start.2 = (f32[1024]{0:T(1024)S(1)}, f32[1024]{0:T(1024)}, u32[]{:S(2)}) copy-start(f32[1024]{0:T(1024)} %param.17) | copy-start | bytes 12292
  19.0 12.2 %collective-permute-start.7 = (bf16[128,256]{1,0:T(8,128)(2,1)S(1)}, bf16[128,256]{1,0:T(8,128)(2,1)S(1)}, u32[]{:S(2)}, u32[]{:S(2)}) collective-permute-start(bf16[128,256]{1,0:T(8,128)(2,1)S(1)} %get-tuple-element.24), channel_id=1, source_target_pairs={{0,24},{4,28},{8,16},{12,20},{16,8},{20,12},{24,0},{28,4},{1,25},{... | collective-permute-start | bytes 196616 | tf_op jit(solution)/shard_map/ppermute | solution.py:620
  21.7 9.5 %collective-permute-start.6 = (bf16[128,256]{1,0:T(8,128)(2,1)S(1)}, bf16[128,256]{1,0:T(8,128)(2,1)S(1)}, u32[]{:S(2)}, u32[]{:S(2)}) collective-permute-start(bf16[128,256]{1,0:T(8,128)(2,1)S(1)} %get-tuple-element.25), channel_id=1, source_target_pairs={{0,16},{4,20},{8,24},{12,28},{16,0},{20,4},{24,8},{28,12},{1,17},{... | collective-permute-start | bytes 196616 | tf_op jit(solution)/shard_map/ppermute | solution.py:620
  22.3 8.9 %collective-permute-start.5 = (bf16[128,256]{1,0:T(8,128)(2,1)S(1)}, bf16[128,256]{1,0:T(8,128)(2,1)S(1)}, u32[]{:S(2)}, u32[]{:S(2)}) collective-permute-start(bf16[128,256]{1,0:T(8,128)(2,1)S(1)} %get-tuple-element.26), channel_id=1, source_target_pairs={{0,8},{4,12},{8,0},{12,4},{16,24},{20,28},{24,16},{28,20},{1,9},{5... | collective-permute-start | bytes 196616 | tf_op jit(solution)/shard_map/ppermute | solution.py:620
  28.9 5.0 %collective-permute-start.9 = (bf16[128,256]{1,0:T(8,128)(2,1)S(1)}, bf16[128,256]{1,0:T(8,128)(2,1)S(1)}, u32[]{:S(2)}, u32[]{:S(2)}) collective-permute-start(bf16[128,256]{1,0:T(8,128)(2,1)S(1)} %get-tuple-element.21), channel_id=1, source_target_pairs={{0,16},{4,20},{8,24},{12,28},{16,0},{20,4},{24,8},{28,12},{1,17},{... | collective-permute-start | bytes 196616 | tf_op jit(solution)/shard_map/ppermute | solution.py:620
  29.8 5.2 %collective-permute-start.8 = (bf16[128,256]{1,0:T(8,128)(2,1)S(1)}, bf16[128,256]{1,0:T(8,128)(2,1)S(1)}, u32[]{:S(2)}, u32[]{:S(2)}) collective-permute-start(bf16[128,256]{1,0:T(8,128)(2,1)S(1)} %get-tuple-element.22), channel_id=1, source_target_pairs={{0,24},{4,28},{8,16},{12,20},{16,8},{20,12},{24,0},{28,4},{1,25},{... | collective-permute-start | bytes 196616 | tf_op jit(solution)/shard_map/ppermute | solution.py:620
  31.2 4.3 %collective-permute-start.10 = (bf16[128,256]{1,0:T(8,128)(2,1)S(1)}, bf16[128,256]{1,0:T(8,128)(2,1)S(1)}, u32[]{:S(2)}, u32[]{:S(2)}) collective-permute-start(bf16[128,256]{1,0:T(8,128)(2,1)S(1)} %held_block.1), channel_id=1, source_target_pairs={{0,8},{4,12},{8,0},{12,4},{16,24},{20,28},{24,16},{28,20},{1,9},{5... | collective-permute-start | bytes 196616 | tf_op jit(solution)/shard_map/ppermute | solution.py:620

commit v3 on v2

--- a/solution.py
+++ b/solution.py
@@ -447,12 +447,16 @@
                     (response[upper, i * width : (i + 1) * width], response[lower, i * width : (i + 1) * width])
                     for i in range(span[-1] + 1 if turn else 1)
                 ]
+                data = {b: (real, imag, real + imag) for b, (real, imag) in data.items()}
+                filt = [(real, imag - real, real + imag) for real, imag in filt]
                 for b in span:
-                    total_real, total_imag = 0.0, 0.0
+                    shared = to_real = to_imag = 0.0
                     for part in range(b + 1 if turn else 1):
-                        (real, imag), (filt_real, filt_imag) = data[b - part], filt[part]
-                        total_real = total_real + (real * filt_real - imag * filt_imag)
-                        total_imag = total_imag + (real * filt_imag + imag * filt_real)
+                        (real, imag, both), (base, ahead, total) = data[b - part], filt[part]
+                        shared = shared + both * base
+                        to_imag = to_imag + real * ahead
+                        to_real = to_real + imag * total
+                    total_real, total_imag = shared - to_real, shared + to_imag
                     sums[b][0].append(total_real)
                     sums[b][1].append(total_imag)
             for b in span:
@@ -592,6 +596,20 @@
 
 def hold_kernel(*refs):
     refs[-1][...] = refs[0][...]
+
+
+def place_part_kernel(*refs, order, extra):
+    blocks, out, sems = refs[extra:-2], refs[-2], refs[-1]
+    span = blocks[0].shape[1]
+    chip = lax.axis_index("seq") // 2
+    copies = []
+    for n, (i, block) in enumerate(zip(order, blocks)):
+        lanes = pl.ds(pl.multiple_of(lax.bitwise_xor(chip, i) * span, span), span)
+        copies.append(pltpu.make_async_copy(block, out.at[:, lanes], sems.at[n]))
+    for copy in copies:
+        copy.start()
+    for copy in copies:
+        copy.wait()
 
 
 def place_kernel(*refs, order):
@@ -694,6 +712,19 @@
             name=name,
         )(*blocks)
 
+    def placed_part(blocks, name, order, so_far=()):
+        return pl.pallas_call(
+            functools.partial(place_part_kernel, order=order, extra=len(so_far)),
+            out_shape=jax.ShapeDtypeStruct((block, width_dev), bf16),
+            in_specs=[in_hbm] * len(so_far) + [whole] * len(blocks),
+            out_specs=in_hbm,
+            scratch_shapes=[pltpu.SemaphoreType.DMA((len(blocks),))],
+            input_output_aliases={0: 0} if so_far else {},
+            compiler_params=params,
+            cost_estimate=pl.CostEstimate(flops=10**9, bytes_accessed=10**6, transcendentals=0),
+            name=name,
+        )(*so_far, *blocks)
+
     def held(value, others):
         return pl.pallas_call(
             hold_kernel,
@@ -727,7 +758,9 @@
     )(hyena, other, all_sums, query_gain.reshape(1, width_dev), key_gain.reshape(1, width_dev))
     last = held(outgoing[order[0]], hyena_parts[1:])
     parts = [outgoing[0]] + [exchange(outgoing[i], 2 * i) for i in order[:0:-1]] + [exchange(last, 2 * order[0])]
-    return placed(hyena_parts, "placed_hyena", order), placed(parts, "placed_attended", order[::-1])
+    early = placed_part(parts[:-1], "placed_early", (0, *order[:0:-1]))
+    attended = placed_part(parts[-1:], "placed_attended", order[:1], (early,))
+    return placed(hyena_parts, "placed_hyena", order), attended
 
 
 def on_device(*operands):

time: 36.5 us -> 36.4 us (level)
  waiting for transfers between devices: 9.07 us -> 8.44 us
  Pallas kernels: 9.36 us -> 9.91 us
    pallas_call x0 -> x2, Pallas kernels: none -> 1.36 us  [placed_part(): pl.pallas_call(functools.partial(place_part_kernel, order=order, extra=le...]
    pallas_call x2 -> x1, Pallas kernels: 1.47 us -> 0.74 us  [placed(): pl.pallas_call(functools.partial(place_kernel, order=(0, *order)), out_sh...]
    ppermute x11, waiting for transfers between devices: 4.36 us -> 3.73 us  [exchange(): lax.ppermute(value, 'seq', [(i, i ^ apart) for i in range(seq_count)])]
  transfers between devices with their start and end apart: 12 -> 12, of which waited for: 6 -> 5; matrix products, arithmetic and copies ran while one was open for 0% -> 0% of each run, Pallas kernels for 13% -> 15%
where the time goes in v3:
time: 36.4 us; the launch traced here: 36.2 us
  starting transfers between devices  17 us (47%)
  Pallas kernels  9.91 us (27%)
  waiting for transfers between devices  8.44 us (23%)
  between operations  0.79 us (2%)
    ppermute x11, starting transfers between devices, exchange(): lax.ppermute(value, 'seq', [(i, i ^ apart) for i in range(seq_count)])  12 us
    all_to_all x1, starting transfers between devices, by_head(): all_sums = lax.all_to_all(square_sums, ('seq', 'ch'), 0, 0, tiled=True)  5.02 us
    all_to_all x1, waiting for transfers between devices, by_head(): all_sums = lax.all_to_all(square_sums, ('seq', 'ch'), 0, 0, tiled=True)  4.71 us
    pallas_call x1, Pallas kernels, by_head(): pl.pallas_call(functools.partial(conv_kernel, piece_count=len(pieces)), o...  3.74 us
    ppermute x11, waiting for transfers between devices, exchange(): lax.ppermute(value, 'seq', [(i, i ^ apart) for i in range(seq_count)])  3.73 us
    pallas_call x1, Pallas kernels, by_head(): pl.pallas_call(functools.partial(attend_kernel, channel_count=width_dev *...  1.59 us
    pallas_call x2, Pallas kernels, placed_part(): pl.pallas_call(functools.partial(place_part_kernel, order=order, extra=le...  1.36 us
    pallas_call x1, Pallas kernels, by_head(): pl.pallas_call(response_kernel, out_shape=[jax.ShapeDtypeStruct((2 * bloc...  1.34 us
  transfers between devices with their start and end apart: 12, of which 5 were waited for; matrix products, arithmetic and copies ran while one was open for 0% of the time, Pallas kernels for 15%

profile of v3, /device:TPU:0, one launch (start us, length us, event | category | flops | bytes accessed | tf_op | source)
XLA Modules:
  0.0 36.2 jit_solution(7582378466766487811)
XLA Ops:
  0.6 0.5 %collective-permute-start = (s32[128]{0:T(128)}, s32[128]{0:T(128)S(1)}, u32[]{:S(2)}, u32[]{:S(2)}) collective-permute-start(s32[128]{0:T(128)} %token_ids.1), channel_id=1, source_target_pairs={{0,4},{4,0},{8,12},{12,8},{16,20},{20,16},{24,28},{28,24},{1,5},{5... | collective-permute-start | bytes 1544 | tf_op jit(solution)/shard_map/ppermute | solution.py:638
  1.1 1.1 %fetched_operands.1 = (s32[128]{0:T(128)S(1)}, f32[16,128]{1,0:T(8,128)S(1)}, f32[16,128]{1,0:T(8,128)S(1)}, f32[128,128]{1,0:T(8,128)S(1)}, bf16[512,256]{1,0:T(8,128)(2,1)S(1)}) custom-call(s32[128]{0:T(128)} %token_ids.1, f32[16,1024]{1,0:T(8,128)} %residue.1, f32[16,1024]{1,0:T(8,128)} %rate.1, f32[128,1024]{1,0:T(8,128)} %medium.1, ...), custom_call_target="tpu_custom_call" | custom-call | flops 1000000000 | bytes 2000000 | tf_op jit(solution)/shard_map/fetched_operands/pallas_call | solution.py:648
  2.2 0.0 collective-permute-done
  2.3 3.6 %collective-permute-start.3 = (s32[2,128]{1,0:T(2,128)S(1)}, s32[2,128]{1,0:T(2,128)S(1)}, u32[]{:S(2)}, u32[]{:S(2)}) collective-permute-start(s32[2,128]{1,0:T(2,128)S(1)} %pad_add_fusion.refs_0_), channel_id=1, source_target_pairs={{0,24},{4,28},{8,16},{12,20},{16,8},{20,12},{24,0},{28,4},{1,25},{... | collective-permute-start | bytes 3080 | tf_op jit(solution)/shard_map/ppermute | solution.py:638
  5.9 0.5 %collective-permute-start.2 = (s32[2,128]{1,0:T(2,128)S(1)}, s32[2,128]{1,0:T(2,128)S(1)}, u32[]{:S(2)}, u32[]{:S(2)}) collective-permute-start(s32[2,128]{1,0:T(2,128)S(1)} %pad_add_fusion.refs_0_), channel_id=1, source_target_pairs={{0,16},{4,20},{8,24},{12,28},{16,0},{20,4},{24,8},{28,12},{1,17},{... | collective-permute-start | bytes 3080 | tf_op jit(solution)/shard_map/ppermute | solution.py:638
  6.4 0.1 collective-permute-start.1
  6.5 0.0 copy-start
  6.5 0.0 copy-start.1
  6.5 0.0 copy-start.4
  6.5 0.0 copy-start.5
  6.5 1.3 %filter_responses.1 = (f32[256,128]{1,0:T(8,128)S(1)}, f32[256,1024]{1,0:T(8,128)S(1)}) custom-call(f32[16,128]{1,0:T(8,128)S(1)} %get-tuple-element.12.residue, f32[16,128]{1,0:T(8,128)S(1)} %get-tuple-element.13.rate, f32[128,128]{1,0:T(8,128)S(1)} %get-tuple-element.14.medium, bf16[512,256]{1,0:T(8,128)(2,1)S(1)} %get-tuple-element.15.table), custom_call_target="tpu_custom_call" | custom-call | flops 2000000000 | bytes 2000000 | tf_op jit(solution)/shard_map/filter_responses/pallas_call | solution.py:666
  7.8 0.0 collective-permute-done.3.refs_3_
  7.9 1.6 %collective-permute-done.2.refs_2_ = s32[2,128]{1,0:T(2,128)S(1)} collective-permute-done((s32[2,128]{1,0:T(2,128)S(1)}, s32[2,128]{1,0:T(2,128)S(1)}, u32[]{:S(2)}, u32[]{:S(2)}) %collective-permute-start.2) | collective-permute-done | bytes 1056 | tf_op jit(solution)/shard_map/ppermute | solution.py:638
  9.4 0.5 %collective-permute-done.1.refs_1_ = s32[2,128]{1,0:T(2,128)S(1)} collective-permute-done((s32[2,128]{1,0:T(2,128)S(1)}, s32[2,128]{1,0:T(2,128)S(1)}, u32[]{:S(2)}, u32[]{:S(2)}) %collective-permute-start.1) | collective-permute-done | bytes 1056 | tf_op jit(solution)/shard_map/ppermute | solution.py:638
  9.9 0.0 copy-done
  9.9 0.0 copy-done.1
  9.9 0.0 copy-done.4
  9.9 0.0 copy-done.5
  10.0 3.7 %gated_convolutions.1 = (bf16[1024,128]{1,0:T(8,128)(2,1)S(1)}, f32[32,8,128]{2,1,0:T(8,128)}) custom-call(s32[2,128]{1,0:T(2,128)S(1)} %pad_add_fusion.refs_0_, s32[2,128]{1,0:T(2,128)S(1)} %collective-permute-done.1.refs_1_, s32[2,128]{1,0:T(2,128)S(1)} %collective-permute-done.2.refs_2_, s32[2,128]{1,0:T(2,128)S(1)} %collective-permute-done.3.refs_3_, ...), custom_call_target="tpu_custom_call" | custom-call | flops 2000000000 | bytes 2000000 | tf_op jit(solution)/shard_map/gated_convolutions/pallas_call | solution.py:680
  13.7 0.1 collective-permute-start.4
  13.8 5.0 %all-to-all-start = ((f32[32,8,128]{2,1,0:T(8,128)}), f32[32,8,128]{2,1,0:T(8,128)S(1)}, u32[]{:S(2)}, u32[]{:S(2)}) async-start(f32[32,8,128]{2,1,0:T(8,128)} %get-tuple-element.19), calls=%async_computation | async-start | bytes 262144 | tf_op jit(solution)/shard_map/all_to_all | solution.py:702
  18.8 0.0 collective-permute-done.4.other
  18.8 0.1 hyena_blocks.1
  18.9 0.0 copy-start.3
  18.9 0.0 copy-start.2
  18.9 2.7 %collective-permute-start.7 = (bf16[128,256]{1,0:T(8,128)(2,1)S(1)}, bf16[128,256]{1,0:T(8,128)(2,1)S(1)}, u32[]{:S(2)}, u32[]{:S(2)}) collective-permute-start(bf16[128,256]{1,0:T(8,128)(2,1)S(1)} %get-tuple-element.24), channel_id=1, source_target_pairs={{0,24},{4,28},{8,16},{12,20},{16,8},{20,12},{24,0},{28,4},{1,25},{... | collective-permute-start | bytes 196616 | tf_op jit(solution)/shard_map/ppermute | solution.py:638
  21.7 0.6 %collective-permute-start.6 = (bf16[128,256]{1,0:T(8,128)(2,1)S(1)}, bf16[128,256]{1,0:T(8,128)(2,1)S(1)}, u32[]{:S(2)}, u32[]{:S(2)}) collective-permute-start(bf16[128,256]{1,0:T(8,128)(2,1)S(1)} %get-tuple-element.25), channel_id=1, source_target_pairs={{0,16},{4,20},{8,24},{12,28},{16,0},{20,4},{24,8},{28,12},{1,17},{... | collective-permute-start | bytes 196616 | tf_op jit(solution)/shard_map/ppermute | solution.py:638
  22.2 0.3 collective-permute-start.5
  22.5 4.7 %all-to-all-done.sums = f32[32,8,128]{2,1,0:T(8,128)S(1)} async-done(((f32[32,8,128]{2,1,0:T(8,128)}), f32[32,8,128]{2,1,0:T(8,128)S(1)}, u32[]{:S(2)}, u32[]{:S(2)}) %all-to-all-start) | async-done | bytes 131104 | tf_op jit(solution)/shard_map/all_to_all | solution.py:702
  27.2 0.0 copy-done.3
  27.2 0.0 copy-done.2
  27.2 1.6 %attention.1 = bf16[4,128,256]{2,1,0:T(8,128)(2,1)S(1)} custom-call(bf16[1024,128]{1,0:T(8,128)(2,1)S(1)} %get-tuple-element.18.own, bf16[1024,128]{1,0:T(8,128)(2,1)S(1)} %collective-permute-done.4.other, f32[32,8,128]{2,1,0:T(8,128)S(1)} %all-to-all-done.sums, f32[1,1024]{1,0:T(1,128)S(1)} %bitcast.21, f32[1,1024]{1,0:T(1,128)S(1)} %bitcast.22), custom_call_target="tpu_custom_call" | custom-call | flops 2000000000 | bytes 1000000 | tf_op jit(solution)/shard_map/attention/pallas_call | solution.py:749
  28.8 0.9 %collective-permute-start.9 = (bf16[128,256]{1,0:T(8,128)(2,1)S(1)}, bf16[128,256]{1,0:T(8,128)(2,1)S(1)}, u32[]{:S(2)}, u32[]{:S(2)}) collective-permute-start(bf16[128,256]{1,0:T(8,128)(2,1)S(1)} %get-tuple-element.21), channel_id=1, source_target_pairs={{0,16},{4,20},{8,24},{12,28},{16,0},{20,4},{24,8},{28,12},{1,17},{... | collective-permute-start | bytes 196616 | tf_op jit(solution)/shard_map/ppermute | solution.py:638
  29.7 1.4 %collective-permute-start.8 = (bf16[128,256]{1,0:T(8,128)(2,1)S(1)}, bf16[128,256]{1,0:T(8,128)(2,1)S(1)}, u32[]{:S(2)}, u32[]{:S(2)}) collective-permute-start(bf16[128,256]{1,0:T(8,128)(2,1)S(1)} %get-tuple-element.22), channel_id=1, source_target_pairs={{0,24},{4,28},{8,16},{12,20},{16,8},{20,12},{24,0},{28,4},{1,25},{... | collective-permute-start | bytes 196616 | tf_op jit(solution)/shard_map/ppermute | solution.py:638
  31.1 0.0 collective-permute-done.7.refs_3_
  31.1 0.0 collective-permute-done.6.refs_2_
  31.1 0.0 collective-permute-done.5.refs_1_
  31.2 1.3 %collective-permute-start.10 = (bf16[128,256]{1,0:T(8,128)(2,1)S(1)}, bf16[128,256]{1,0:T(8,128)(2,1)S(1)}, u32[]{:S(2)}, u32[]{:S(2)}) collective-permute-start(bf16[128,256]{1,0:T(8,128)(2,1)S(1)} %held_block.1), channel_id=1, source_target_pairs={{0,8},{4,12},{8,0},{12,4},{16,24},{20,28},{24,16},{28,20},{1,9},{5... | collective-permute-start | bytes 196616 | tf_op jit(solution)/shard_map/ppermute | solution.py:638
  32.5 0.7 %placed_hyena.1 = bf16[128,1024]{1,0:T(8,128)(2,1)} custom-call(bf16[128,256]{1,0:T(8,128)(2,1)S(1)} %get-tuple-element.27.refs_0_, bf16[128,256]{1,0:T(8,128)(2,1)S(1)} %collective-permute-done.5.refs_1_, bf16[128,256]{1,0:T(8,128)(2,1)S(1)} %collective-permute-done.6.refs_2_, bf16[128,256]{1,0:T(8,128)(2,1)S(1)} %collective-permute-done.7.refs_3_), custom_call_target="tpu_custom_call" | custom-call | flops 1000000000 | bytes 1000000 | tf_op jit(solution)/shard_map/placed_hyena/pallas_call | solution.py:705
  33.2 0.6 %collective-permute-done.9.refs_2_ = bf16[128,256]{1,0:T(8,128)(2,1)S(1)} collective-permute-done((bf16[128,256]{1,0:T(8,128)(2,1)S(1)}, bf16[128,256]{1,0:T(8,128)(2,1)S(1)}, u32[]{:S(2)}, u32[]{:S(2)}) %collective-permute-start.9) | collective-permute-done | bytes 65568 | tf_op jit(solution)/shard_map/ppermute | solution.py:638
  33.9 1.0 %collective-permute-done.8.refs_1_ = bf16[128,256]{1,0:T(8,128)(2,1)S(1)} collective-permute-done((bf16[128,256]{1,0:T(8,128)(2,1)S(1)}, bf16[128,256]{1,0:T(8,128)(2,1)S(1)}, u32[]{:S(2)}, u32[]{:S(2)}) %collective-permute-start.8) | collective-permute-done | bytes 65568 | tf_op jit(solution)/shard_map/ppermute | solution.py:638
  34.8 0.7 %placed_early.1.refs_0_ = bf16[128,1024]{1,0:T(8,128)(2,1)} custom-call(bf16[128,256]{1,0:T(8,128)(2,1)S(1)} %get-tuple-element.23.refs_0_, bf16[128,256]{1,0:T(8,128)(2,1)S(1)} %collective-permute-done.8.refs_1_, bf16[128,256]{1,0:T(8,128)(2,1)S(1)} %collective-permute-done.9.refs_2_), custom_call_target="tpu_custom_call" | custom-call | flops 1000000000 | bytes 1000000 | tf_op jit(solution)/shard_map/placed_early/pallas_call | solution.py:716
  35.6 0.0 collective-permute-done.10.refs_1_
  35.6 0.7 %placed_attended.1 = bf16[128,1024]{1,0:T(8,128)(2,1)} custom-call(bf16[128,1024]{1,0:T(8,128)(2,1)} %placed_early.1.refs_0_, bf16[128,256]{1,0:T(8,128)(2,1)S(1)} %collective-permute-done.10.refs_1_), custom_call_target="tpu_custom_call", output_to_operand_aliasing={{}: (0, {})} | custom-call | flops 1000000000 | bytes 1000000 | tf_op jit(solution)/shard_map/placed_attended/pallas_call | solution.py:716
  (4 shorter events, 0.1 us)
Async XLA Ops:
  0.6 1.6 %collective-permute-start = (s32[128]{0:T(128)}, s32[128]{0:T(128)S(1)}, u32[]{:S(2)}, u32[]{:S(2)}) collective-permute-start(s32[128]{0:T(128)} %token_ids.1), channel_id=1, source_target_pairs={{0,4},{4,0},{8,12},{12,8},{16,20},{20,16},{24,28},{28,24},{1,5},{5... | collective-permute-start | bytes 1544 | tf_op jit(solution)/shard_map/ppermute | solution.py:638
  2.3 5.6 %collective-permute-start.3 = (s32[2,128]{1,0:T(2,128)S(1)}, s32[2,128]{1,0:T(2,128)S(1)}, u32[]{:S(2)}, u32[]{:S(2)}) collective-permute-start(s32[2,128]{1,0:T(2,128)S(1)} %pad_add_fusion.refs_0_), channel_id=1, source_target_pairs={{0,24},{4,28},{8,16},{12,20},{16,8},{20,12},{24,0},{28,4},{1,25},{... | collective-permute-start | bytes 3080 | tf_op jit(solution)/shard_map/ppermute | solution.py:638
  5.9 3.6 %collective-permute-start.2 = (s32[2,128]{1,0:T(2,128)S(1)}, s32[2,128]{1,0:T(2,128)S(1)}, u32[]{:S(2)}, u32[]{:S(2)}) collective-permute-start(s32[2,128]{1,0:T(2,128)S(1)} %pad_add_fusion.refs_0_), channel_id=1, source_target_pairs={{0,16},{4,20},{8,24},{12,28},{16,0},{20,4},{24,8},{28,12},{1,17},{... | collective-permute-start | bytes 3080 | tf_op jit(solution)/shard_map/ppermute | solution.py:638
  6.4 3.6 %collective-permute-start.1 = (s32[2,128]{1,0:T(2,128)S(1)}, s32[2,128]{1,0:T(2,128)S(1)}, u32[]{:S(2)}, u32[]{:S(2)}) collective-permute-start(s32[2,128]{1,0:T(2,128)S(1)} %pad_add_fusion.refs_0_), channel_id=1, source_target_pairs={{0,8},{4,12},{8,0},{12,4},{16,24},{20,28},{24,16},{28,20},{1,9},{5... | collective-permute-start | bytes 3080 | tf_op jit(solution)/shard_map/ppermute | solution.py:638
  6.5 3.4 %copy-start = (bf16[512,1024]{1,0:T(8,128)(2,1)S(1)}, bf16[512,1024]{1,0:T(8,128)(2,1)}, u32[]{:S(2)}) copy-start(bf16[512,1024]{1,0:T(8,128)(2,1)} %refs_4_.1) | copy-start | bytes 3145732
  6.5 3.4 %copy-start.1 = (f32[7,1024]{1,0:T(8,128)S(1)}, f32[7,1024]{1,0:T(8,128)}, u32[]{:S(2)}) copy-start(f32[7,1024]{1,0:T(8,128)} %refs_5_.1) | copy-start | bytes 86020
  6.5 3.4 %copy-start.4 = (bf16[128,1536]{1,0:T(8,128)(2,1)S(1)}, bf16[128,1536]{1,0:T(8,128)(2,1)}, u32[]{:S(2)}) copy-start(bf16[128,1536]{1,0:T(8,128)(2,1)} %constant.8.clone.refs_9_) | copy-start | bytes 1179652
  6.5 3.4 %copy-start.5 = (bf16[256,768]{1,0:T(8,128)(2,1)S(1)}, bf16[256,768]{1,0:T(8,128)(2,1)}, u32[]{:S(2)}) copy-start(bf16[256,768]{1,0:T(8,128)(2,1)} %constant.7.clone.refs_8_) | copy-start | bytes 1179652
  13.7 5.1 %collective-permute-start.4 = (bf16[1024,128]{1,0:T(8,128)(2,1)S(1)}, bf16[1024,128]{1,0:T(8,128)(2,1)S(1)}, u32[]{:S(2)}, u32[]{:S(2)}) collective-permute-start(bf16[1024,128]{1,0:T(8,128)(2,1)S(1)} %get-tuple-element.18.own), channel_id=1, source_target_pairs={{0,4},{4,0},{8,12},{12,8},{16,20},{20,16},{24,28},{28,24},{1,5},{5... | collective-permute-start | bytes 786440 | tf_op jit(solution)/shard_map/ppermute | solution.py:638
  13.8 13.4 %all-to-all-start = ((f32[32,8,128]{2,1,0:T(8,128)}), f32[32,8,128]{2,1,0:T(8,128)S(1)}, u32[]{:S(2)}, u32[]{:S(2)}) async-start(f32[32,8,128]{2,1,0:T(8,128)} %get-tuple-element.19), calls=%async_computation | async-start | bytes 262144 | tf_op jit(solution)/shard_map/all_to_all | solution.py:702
  18.9 8.3 %copy-start.3 = (f32[1024]{0:T(1024)S(1)}, f32[1024]{0:T(1024)}, u32[]{:S(2)}) copy-start(f32[1024]{0:T(1024)} %param.18) | copy-start | bytes 12292
  18.9 8.3 %copy-start.2 = (f32[1024]{0:T(1024)S(1)}, f32[1024]{0:T(1024)}, u32[]{:S(2)}) copy-start(f32[1024]{0:T(1024)} %param.17) | copy-start | bytes 12292
  18.9 12.2 %collective-permute-start.7 = (bf16[128,256]{1,0:T(8,128)(2,1)S(1)}, bf16[128,256]{1,0:T(8,128)(2,1)S(1)}, u32[]{:S(2)}, u32[]{:S(2)}) collective-permute-start(bf16[128,256]{1,0:T(8,128)(2,1)S(1)} %get-tuple-element.24), channel_id=1, source_target_pairs={{0,24},{4,28},{8,16},{12,20},{16,8},{20,12},{24,0},{28,4},{1,25},{... | collective-permute-start | bytes 196616 | tf_op jit(solution)/shard_map/ppermute | solution.py:638
  21.7 9.5 %collective-permute-start.6 = (bf16[128,256]{1,0:T(8,128)(2,1)S(1)}, bf16[128,256]{1,0:T(8,128)(2,1)S(1)}, u32[]{:S(2)}, u32[]{:S(2)}) collective-permute-start(bf16[128,256]{1,0:T(8,128)(2,1)S(1)} %get-tuple-element.25), channel_id=1, source_target_pairs={{0,16},{4,20},{8,24},{12,28},{16,0},{20,4},{24,8},{28,12},{1,17},{... | collective-permute-start | bytes 196616 | tf_op jit(solution)/shard_map/ppermute | solution.py:638
  22.2 8.9 %collective-permute-start.5 = (bf16[128,256]{1,0:T(8,128)(2,1)S(1)}, bf16[128,256]{1,0:T(8,128)(2,1)S(1)}, u32[]{:S(2)}, u32[]{:S(2)}) collective-permute-start(bf16[128,256]{1,0:T(8,128)(2,1)S(1)} %get-tuple-element.26), channel_id=1, source_target_pairs={{0,8},{4,12},{8,0},{12,4},{16,24},{20,28},{24,16},{28,20},{1,9},{5... | collective-permute-start | bytes 196616 | tf_op jit(solution)/shard_map/ppermute | solution.py:638
  28.8 5.0 %collective-permute-start.9 = (bf16[128,256]{1,0:T(8,128)(2,1)S(1)}, bf16[128,256]{1,0:T(8,128)(2,1)S(1)}, u32[]{:S(2)}, u32[]{:S(2)}) collective-permute-start(bf16[128,256]{1,0:T(8,128)(2,1)S(1)} %get-tuple-element.21), channel_id=1, source_target_pairs={{0,16},{4,20},{8,24},{12,28},{16,0},{20,4},{24,8},{28,12},{1,17},{... | collective-permute-start | bytes 196616 | tf_op jit(solution)/shard_map/ppermute | solution.py:638
  29.7 5.2 %collective-permute-start.8 = (bf16[128,256]{1,0:T(8,128)(2,1)S(1)}, bf16[128,256]{1,0:T(8,128)(2,1)S(1)}, u32[]{:S(2)}, u32[]{:S(2)}) collective-permute-start(bf16[128,256]{1,0:T(8,128)(2,1)S(1)} %get-tuple-element.22), channel_id=1, source_target_pairs={{0,24},{4,28},{8,16},{12,20},{16,8},{20,12},{24,0},{28,4},{1,25},{... | collective-permute-start | bytes 196616 | tf_op jit(solution)/shard_map/ppermute | solution.py:638
  31.2 4.4 %collective-permute-start.10 = (bf16[128,256]{1,0:T(8,128)(2,1)S(1)}, bf16[128,256]{1,0:T(8,128)(2,1)S(1)}, u32[]{:S(2)}, u32[]{:S(2)}) collective-permute-start(bf16[128,256]{1,0:T(8,128)(2,1)S(1)} %held_block.1), channel_id=1, source_target_pairs={{0,8},{4,12},{8,0},{12,4},{16,24},{20,28},{24,16},{28,20},{1,9},{5... | collective-permute-start | bytes 196616 | tf_op jit(solution)/shard_map/ppermute | solution.py:638

commit v4 on v3

--- a/solution.py
+++ b/solution.py
@@ -571,15 +571,15 @@
 
     for b in range(count):
         normalise(b)
-    chains = [(chip, side) for chip in range(count // 2) for side in range(2)]
+    chains = [(chip, side) for chip in reversed(range(count // 2)) for side in range(2)]
     scored, weighed = {}, {}
-    for turn in range(len(chains) + 2):
+    for turn in range(len(chains) + 4):
         if turn < len(chains):
             scored[turn] = score(*chains[turn])
-        if 0 <= turn - 1 < len(chains):
-            weighed[turn - 1] = weigh(scored.pop(turn - 1))
         if 0 <= turn - 2 < len(chains):
-            blend(*chains[turn - 2], *weighed.pop(turn - 2))
+            weighed[turn - 2] = weigh(scored.pop(turn - 2))
+        if 0 <= turn - 4 < len(chains):
+            blend(*chains[turn - 4], *weighed.pop(turn - 4))
 
 
 def outgoing_kernel(own, other, out):

time: 36.4 us -> 36.3 us (level)
  no operation moved by 1% of the time
where the time goes in v4:
time: 36.3 us; the launch traced here: 36.1 us
  starting transfers between devices  17 us (47%)
  Pallas kernels  9.77 us (27%)
  waiting for transfers between devices  8.44 us (23%)
  between operations  0.79 us (2%)
    ppermute x11, starting transfers between devices, exchange(): lax.ppermute(value, 'seq', [(i, i ^ apart) for i in range(seq_count)])  12 us
    all_to_all x1, starting transfers between devices, by_head(): all_sums = lax.all_to_all(square_sums, ('seq', 'ch'), 0, 0, tiled=True)  5.02 us
    all_to_all x1, waiting for transfers between devices, by_head(): all_sums = lax.all_to_all(square_sums, ('seq', 'ch'), 0, 0, tiled=True)  4.71 us
    pallas_call x1, Pallas kernels, by_head(): pl.pallas_call(functools.partial(conv_kernel, piece_count=len(pieces)), o...  3.74 us
    ppermute x11, waiting for transfers between devices, exchange(): lax.ppermute(value, 'seq', [(i, i ^ apart) for i in range(seq_count)])  3.73 us
    pallas_call x1, Pallas kernels, by_head(): pl.pallas_call(functools.partial(attend_kernel, channel_count=width_dev *...  1.45 us
    pallas_call x2, Pallas kernels, placed_part(): pl.pallas_call(functools.partial(place_part_kernel, order=order, extra=le...  1.36 us
    pallas_call x1, Pallas kernels, by_head(): pl.pallas_call(response_kernel, out_shape=[jax.ShapeDtypeStruct((2 * bloc...  1.34 us
  transfers between devices with their start and end apart: 12, of which 5 were waited for; matrix products, arithmetic and copies ran while one was open for 0% of the time, Pallas kernels for 15%

profile of v4, /device:TPU:0, one launch (start us, length us, event | category | flops | bytes accessed | tf_op | source)
XLA Modules:
  0.0 36.1 jit_solution(10919522119183179533)
XLA Ops:
  0.6 0.5 %collective-permute-start = (s32[128]{0:T(128)}, s32[128]{0:T(128)S(1)}, u32[]{:S(2)}, u32[]{:S(2)}) collective-permute-start(s32[128]{0:T(128)} %token_ids.1), channel_id=1, source_target_pairs={{0,4},{4,0},{8,12},{12,8},{16,20},{20,16},{24,28},{28,24},{1,5},{5... | collective-permute-start | bytes 1544 | tf_op jit(solution)/shard_map/ppermute | solution.py:638
  1.1 1.1 %fetched_operands.1 = (s32[128]{0:T(128)S(1)}, f32[16,128]{1,0:T(8,128)S(1)}, f32[16,128]{1,0:T(8,128)S(1)}, f32[128,128]{1,0:T(8,128)S(1)}, bf16[512,256]{1,0:T(8,128)(2,1)S(1)}) custom-call(s32[128]{0:T(128)} %token_ids.1, f32[16,1024]{1,0:T(8,128)} %residue.1, f32[16,1024]{1,0:T(8,128)} %rate.1, f32[128,1024]{1,0:T(8,128)} %medium.1, ...), custom_call_target="tpu_custom_call" | custom-call | flops 1000000000 | bytes 2000000 | tf_op jit(solution)/shard_map/fetched_operands/pallas_call | solution.py:648
  2.2 0.0 collective-permute-done
  2.3 3.6 %collective-permute-start.3 = (s32[2,128]{1,0:T(2,128)S(1)}, s32[2,128]{1,0:T(2,128)S(1)}, u32[]{:S(2)}, u32[]{:S(2)}) collective-permute-start(s32[2,128]{1,0:T(2,128)S(1)} %pad_add_fusion.refs_0_), channel_id=1, source_target_pairs={{0,24},{4,28},{8,16},{12,20},{16,8},{20,12},{24,0},{28,4},{1,25},{... | collective-permute-start | bytes 3080 | tf_op jit(solution)/shard_map/ppermute | solution.py:638
  5.9 0.5 %collective-permute-start.2 = (s32[2,128]{1,0:T(2,128)S(1)}, s32[2,128]{1,0:T(2,128)S(1)}, u32[]{:S(2)}, u32[]{:S(2)}) collective-permute-start(s32[2,128]{1,0:T(2,128)S(1)} %pad_add_fusion.refs_0_), channel_id=1, source_target_pairs={{0,16},{4,20},{8,24},{12,28},{16,0},{20,4},{24,8},{28,12},{1,17},{... | collective-permute-start | bytes 3080 | tf_op jit(solution)/shard_map/ppermute | solution.py:638
  6.4 0.1 collective-permute-start.1
  6.5 0.0 copy-start
  6.5 0.0 copy-start.1
  6.5 0.0 copy-start.4
  6.5 0.0 copy-start.5
  6.5 1.3 %filter_responses.1 = (f32[256,128]{1,0:T(8,128)S(1)}, f32[256,1024]{1,0:T(8,128)S(1)}) custom-call(f32[16,128]{1,0:T(8,128)S(1)} %get-tuple-element.12.residue, f32[16,128]{1,0:T(8,128)S(1)} %get-tuple-element.13.rate, f32[128,128]{1,0:T(8,128)S(1)} %get-tuple-element.14.medium, bf16[512,256]{1,0:T(8,128)(2,1)S(1)} %get-tuple-element.15.table), custom_call_target="tpu_custom_call" | custom-call | flops 2000000000 | bytes 2000000 | tf_op jit(solution)/shard_map/filter_responses/pallas_call | solution.py:666
  7.8 0.0 collective-permute-done.3.refs_3_
  7.9 1.6 %collective-permute-done.2.refs_2_ = s32[2,128]{1,0:T(2,128)S(1)} collective-permute-done((s32[2,128]{1,0:T(2,128)S(1)}, s32[2,128]{1,0:T(2,128)S(1)}, u32[]{:S(2)}, u32[]{:S(2)}) %collective-permute-start.2) | collective-permute-done | bytes 1056 | tf_op jit(solution)/shard_map/ppermute | solution.py:638
  9.4 0.5 %collective-permute-done.1.refs_1_ = s32[2,128]{1,0:T(2,128)S(1)} collective-permute-done((s32[2,128]{1,0:T(2,128)S(1)}, s32[2,128]{1,0:T(2,128)S(1)}, u32[]{:S(2)}, u32[]{:S(2)}) %collective-permute-start.1) | collective-permute-done | bytes 1056 | tf_op jit(solution)/shard_map/ppermute | solution.py:638
  9.9 0.0 copy-done
  9.9 0.0 copy-done.1
  9.9 0.0 copy-done.4
  9.9 0.0 copy-done.5
  10.0 3.7 %gated_convolutions.1 = (bf16[1024,128]{1,0:T(8,128)(2,1)S(1)}, f32[32,8,128]{2,1,0:T(8,128)}) custom-call(s32[2,128]{1,0:T(2,128)S(1)} %pad_add_fusion.refs_0_, s32[2,128]{1,0:T(2,128)S(1)} %collective-permute-done.1.refs_1_, s32[2,128]{1,0:T(2,128)S(1)} %collective-permute-done.2.refs_2_, s32[2,128]{1,0:T(2,128)S(1)} %collective-permute-done.3.refs_3_, ...), custom_call_target="tpu_custom_call" | custom-call | flops 2000000000 | bytes 2000000 | tf_op jit(solution)/shard_map/gated_convolutions/pallas_call | solution.py:680
  13.7 0.1 collective-permute-start.4
  13.8 5.0 %all-to-all-start = ((f32[32,8,128]{2,1,0:T(8,128)}), f32[32,8,128]{2,1,0:T(8,128)S(1)}, u32[]{:S(2)}, u32[]{:S(2)}) async-start(f32[32,8,128]{2,1,0:T(8,128)} %get-tuple-element.19), calls=%async_computation | async-start | bytes 262144 | tf_op jit(solution)/shard_map/all_to_all | solution.py:702
  18.8 0.0 collective-permute-done.4.other
  18.8 0.1 hyena_blocks.1
  18.9 0.0 copy-start.3
  18.9 0.0 copy-start.2
  18.9 2.7 %collective-permute-start.7 = (bf16[128,256]{1,0:T(8,128)(2,1)S(1)}, bf16[128,256]{1,0:T(8,128)(2,1)S(1)}, u32[]{:S(2)}, u32[]{:S(2)}) collective-permute-start(bf16[128,256]{1,0:T(8,128)(2,1)S(1)} %get-tuple-element.24), channel_id=1, source_target_pairs={{0,24},{4,28},{8,16},{12,20},{16,8},{20,12},{24,0},{28,4},{1,25},{... | collective-permute-start | bytes 196616 | tf_op jit(solution)/shard_map/ppermute | solution.py:638
  21.7 0.6 %collective-permute-start.6 = (bf16[128,256]{1,0:T(8,128)(2,1)S(1)}, bf16[128,256]{1,0:T(8,128)(2,1)S(1)}, u32[]{:S(2)}, u32[]{:S(2)}) collective-permute-start(bf16[128,256]{1,0:T(8,128)(2,1)S(1)} %get-tuple-element.25), channel_id=1, source_target_pairs={{0,16},{4,20},{8,24},{12,28},{16,0},{20,4},{24,8},{28,12},{1,17},{... | collective-permute-start | bytes 196616 | tf_op jit(solution)/shard_map/ppermute | solution.py:638
  22.2 0.3 collective-permute-start.5
  22.5 4.7 %all-to-all-done.sums = f32[32,8,128]{2,1,0:T(8,128)S(1)} async-done(((f32[32,8,128]{2,1,0:T(8,128)}), f32[32,8,128]{2,1,0:T(8,128)S(1)}, u32[]{:S(2)}, u32[]{:S(2)}) %all-to-all-start) | async-done | bytes 131104 | tf_op jit(solution)/shard_map/all_to_all | solution.py:702
  27.2 0.0 copy-done.3
  27.2 0.0 copy-done.2
  27.2 1.5 %attention.1 = bf16[4,128,256]{2,1,0:T(8,128)(2,1)S(1)} custom-call(bf16[1024,128]{1,0:T(8,128)(2,1)S(1)} %get-tuple-element.18.own, bf16[1024,128]{1,0:T(8,128)(2,1)S(1)} %collective-permute-done.4.other, f32[32,8,128]{2,1,0:T(8,128)S(1)} %all-to-all-done.sums, f32[1,1024]{1,0:T(1,128)S(1)} %bitcast.21, f32[1,1024]{1,0:T(1,128)S(1)} %bitcast.22), custom_call_target="tpu_custom_call" | custom-call | flops 2000000000 | bytes 1000000 | tf_op jit(solution)/shard_map/attention/pallas_call | solution.py:749
  28.7 0.9 %collective-permute-start.9 = (bf16[128,256]{1,0:T(8,128)(2,1)S(1)}, bf16[128,256]{1,0:T(8,128)(2,1)S(1)}, u32[]{:S(2)}, u32[]{:S(2)}) collective-permute-start(bf16[128,256]{1,0:T(8,128)(2,1)S(1)} %get-tuple-element.21), channel_id=1, source_target_pairs={{0,16},{4,20},{8,24},{12,28},{16,0},{20,4},{24,8},{28,12},{1,17},{... | collective-permute-start | bytes 196616 | tf_op jit(solution)/shard_map/ppermute | solution.py:638
  29.6 1.4 %collective-permute-start.8 = (bf16[128,256]{1,0:T(8,128)(2,1)S(1)}, bf16[128,256]{1,0:T(8,128)(2,1)S(1)}, u32[]{:S(2)}, u32[]{:S(2)}) collective-permute-start(bf16[128,256]{1,0:T(8,128)(2,1)S(1)} %get-tuple-element.22), channel_id=1, source_target_pairs={{0,24},{4,28},{8,16},{12,20},{16,8},{20,12},{24,0},{28,4},{1,25},{... | collective-permute-start | bytes 196616 | tf_op jit(solution)/shard_map/ppermute | solution.py:638
  31.0 0.0 collective-permute-done.7.refs_3_
  31.0 0.0 collective-permute-done.6.refs_2_
  31.0 0.0 collective-permute-done.5.refs_1_
  31.0 1.3 %collective-permute-start.10 = (bf16[128,256]{1,0:T(8,128)(2,1)S(1)}, bf16[128,256]{1,0:T(8,128)(2,1)S(1)}, u32[]{:S(2)}, u32[]{:S(2)}) collective-permute-start(bf16[128,256]{1,0:T(8,128)(2,1)S(1)} %held_block.1), channel_id=1, source_target_pairs={{0,8},{4,12},{8,0},{12,4},{16,24},{20,28},{24,16},{28,20},{1,9},{5... | collective-permute-start | bytes 196616 | tf_op jit(solution)/shard_map/ppermute | solution.py:638
  32.3 0.7 %placed_hyena.1 = bf16[128,1024]{1,0:T(8,128)(2,1)} custom-call(bf16[128,256]{1,0:T(8,128)(2,1)S(1)} %get-tuple-element.27.refs_0_, bf16[128,256]{1,0:T(8,128)(2,1)S(1)} %collective-permute-done.5.refs_1_, bf16[128,256]{1,0:T(8,128)(2,1)S(1)} %collective-permute-done.6.refs_2_, bf16[128,256]{1,0:T(8,128)(2,1)S(1)} %collective-permute-done.7.refs_3_), custom_call_target="tpu_custom_call" | custom-call | flops 1000000000 | bytes 1000000 | tf_op jit(solution)/shard_map/placed_hyena/pallas_call | solution.py:705
  33.1 0.6 %collective-permute-done.9.refs_2_ = bf16[128,256]{1,0:T(8,128)(2,1)S(1)} collective-permute-done((bf16[128,256]{1,0:T(8,128)(2,1)S(1)}, bf16[128,256]{1,0:T(8,128)(2,1)S(1)}, u32[]{:S(2)}, u32[]{:S(2)}) %collective-permute-start.9) | collective-permute-done | bytes 65568 | tf_op jit(solution)/shard_map/ppermute | solution.py:638
  33.7 1.0 %collective-permute-done.8.refs_1_ = bf16[128,256]{1,0:T(8,128)(2,1)S(1)} collective-permute-done((bf16[128,256]{1,0:T(8,128)(2,1)S(1)}, bf16[128,256]{1,0:T(8,128)(2,1)S(1)}, u32[]{:S(2)}, u32[]{:S(2)}) %collective-permute-start.8) | collective-permute-done | bytes 65568 | tf_op jit(solution)/shard_map/ppermute | solution.py:638
  34.7 0.7 %placed_early.1.refs_0_ = bf16[128,1024]{1,0:T(8,128)(2,1)} custom-call(bf16[128,256]{1,0:T(8,128)(2,1)S(1)} %get-tuple-element.23.refs_0_, bf16[128,256]{1,0:T(8,128)(2,1)S(1)} %collective-permute-done.8.refs_1_, bf16[128,256]{1,0:T(8,128)(2,1)S(1)} %collective-permute-done.9.refs_2_), custom_call_target="tpu_custom_call" | custom-call | flops 1000000000 | bytes 1000000 | tf_op jit(solution)/shard_map/placed_early/pallas_call | solution.py:716
  35.4 0.0 collective-permute-done.10.refs_1_
  35.4 0.7 %placed_attended.1 = bf16[128,1024]{1,0:T(8,128)(2,1)} custom-call(bf16[128,1024]{1,0:T(8,128)(2,1)} %placed_early.1.refs_0_, bf16[128,256]{1,0:T(8,128)(2,1)S(1)} %collective-permute-done.10.refs_1_), custom_call_target="tpu_custom_call", output_to_operand_aliasing={{}: (0, {})} | custom-call | flops 1000000000 | bytes 1000000 | tf_op jit(solution)/shard_map/placed_attended/pallas_call | solution.py:716
  (4 shorter events, 0.1 us)
Async XLA Ops:
  0.6 1.6 %collective-permute-start = (s32[128]{0:T(128)}, s32[128]{0:T(128)S(1)}, u32[]{:S(2)}, u32[]{:S(2)}) collective-permute-start(s32[128]{0:T(128)} %token_ids.1), channel_id=1, source_target_pairs={{0,4},{4,0},{8,12},{12,8},{16,20},{20,16},{24,28},{28,24},{1,5},{5... | collective-permute-start | bytes 1544 | tf_op jit(solution)/shard_map/ppermute | solution.py:638
  2.3 5.6 %collective-permute-start.3 = (s32[2,128]{1,0:T(2,128)S(1)}, s32[2,128]{1,0:T(2,128)S(1)}, u32[]{:S(2)}, u32[]{:S(2)}) collective-permute-start(s32[2,128]{1,0:T(2,128)S(1)} %pad_add_fusion.refs_0_), channel_id=1, source_target_pairs={{0,24},{4,28},{8,16},{12,20},{16,8},{20,12},{24,0},{28,4},{1,25},{... | collective-permute-start | bytes 3080 | tf_op jit(solution)/shard_map/ppermute | solution.py:638
  5.9 3.6 %collective-permute-start.2 = (s32[2,128]{1,0:T(2,128)S(1)}, s32[2,128]{1,0:T(2,128)S(1)}, u32[]{:S(2)}, u32[]{:S(2)}) collective-permute-start(s32[2,128]{1,0:T(2,128)S(1)} %pad_add_fusion.refs_0_), channel_id=1, source_target_pairs={{0,16},{4,20},{8,24},{12,28},{16,0},{20,4},{24,8},{28,12},{1,17},{... | collective-permute-start | bytes 3080 | tf_op jit(solution)/shard_map/ppermute | solution.py:638
  6.4 3.6 %collective-permute-start.1 = (s32[2,128]{1,0:T(2,128)S(1)}, s32[2,128]{1,0:T(2,128)S(1)}, u32[]{:S(2)}, u32[]{:S(2)}) collective-permute-start(s32[2,128]{1,0:T(2,128)S(1)} %pad_add_fusion.refs_0_), channel_id=1, source_target_pairs={{0,8},{4,12},{8,0},{12,4},{16,24},{20,28},{24,16},{28,20},{1,9},{5... | collective-permute-start | bytes 3080 | tf_op jit(solution)/shard_map/ppermute | solution.py:638
  6.5 3.4 %copy-start = (bf16[512,1024]{1,0:T(8,128)(2,1)S(1)}, bf16[512,1024]{1,0:T(8,128)(2,1)}, u32[]{:S(2)}) copy-start(bf16[512,1024]{1,0:T(8,128)(2,1)} %refs_4_.1) | copy-start | bytes 3145732
  6.5 3.4 %copy-start.1 = (f32[7,1024]{1,0:T(8,128)S(1)}, f32[7,1024]{1,0:T(8,128)}, u32[]{:S(2)}) copy-start(f32[7,1024]{1,0:T(8,128)} %refs_5_.1) | copy-start | bytes 86020
  6.5 3.4 %copy-start.4 = (bf16[128,1536]{1,0:T(8,128)(2,1)S(1)}, bf16[128,1536]{1,0:T(8,128)(2,1)}, u32[]{:S(2)}) copy-start(bf16[128,1536]{1,0:T(8,128)(2,1)} %constant.8.clone.refs_9_) | copy-start | bytes 1179652
  6.5 3.4 %copy-start.5 = (bf16[256,768]{1,0:T(8,128)(2,1)S(1)}, bf16[256,768]{1,0:T(8,128)(2,1)}, u32[]{:S(2)}) copy-start(bf16[256,768]{1,0:T(8,128)(2,1)} %constant.7.clone.refs_8_) | copy-start | bytes 1179652
  13.7 5.1 %collective-permute-start.4 = (bf16[1024,128]{1,0:T(8,128)(2,1)S(1)}, bf16[1024,128]{1,0:T(8,128)(2,1)S(1)}, u32[]{:S(2)}, u32[]{:S(2)}) collective-permute-start(bf16[1024,128]{1,0:T(8,128)(2,1)S(1)} %get-tuple-element.18.own), channel_id=1, source_target_pairs={{0,4},{4,0},{8,12},{12,8},{16,20},{20,16},{24,28},{28,24},{1,5},{5... | collective-permute-start | bytes 786440 | tf_op jit(solution)/shard_map/ppermute | solution.py:638
  13.8 13.4 %all-to-all-start = ((f32[32,8,128]{2,1,0:T(8,128)}), f32[32,8,128]{2,1,0:T(8,128)S(1)}, u32[]{:S(2)}, u32[]{:S(2)}) async-start(f32[32,8,128]{2,1,0:T(8,128)} %get-tuple-element.19), calls=%async_computation | async-start | bytes 262144 | tf_op jit(solution)/shard_map/all_to_all | solution.py:702
  18.9 8.3 %copy-start.3 = (f32[1024]{0:T(1024)S(1)}, f32[1024]{0:T(1024)}, u32[]{:S(2)}) copy-start(f32[1024]{0:T(1024)} %param.18) | copy-start | bytes 12292
  18.9 8.3 %copy-start.2 = (f32[1024]{0:T(1024)S(1)}, f32[1024]{0:T(1024)}, u32[]{:S(2)}) copy-start(f32[1024]{0:T(1024)} %param.17) | copy-start | bytes 12292
  18.9 12.1 %collective-permute-start.7 = (bf16[128,256]{1,0:T(8,128)(2,1)S(1)}, bf16[128,256]{1,0:T(8,128)(2,1)S(1)}, u32[]{:S(2)}, u32[]{:S(2)}) collective-permute-start(bf16[128,256]{1,0:T(8,128)(2,1)S(1)} %get-tuple-element.24), channel_id=1, source_target_pairs={{0,24},{4,28},{8,16},{12,20},{16,8},{20,12},{24,0},{28,4},{1,25},{... | collective-permute-start | bytes 196616 | tf_op jit(solution)/shard_map/ppermute | solution.py:638
  21.7 9.3 %collective-permute-start.6 = (bf16[128,256]{1,0:T(8,128)(2,1)S(1)}, bf16[128,256]{1,0:T(8,128)(2,1)S(1)}, u32[]{:S(2)}, u32[]{:S(2)}) collective-permute-start(bf16[128,256]{1,0:T(8,128)(2,1)S(1)} %get-tuple-element.25), channel_id=1, source_target_pairs={{0,16},{4,20},{8,24},{12,28},{16,0},{20,4},{24,8},{28,12},{1,17},{... | collective-permute-start | bytes 196616 | tf_op jit(solution)/shard_map/ppermute | solution.py:638
  22.2 8.8 %collective-permute-start.5 = (bf16[128,256]{1,0:T(8,128)(2,1)S(1)}, bf16[128,256]{1,0:T(8,128)(2,1)S(1)}, u32[]{:S(2)}, u32[]{:S(2)}) collective-permute-start(bf16[128,256]{1,0:T(8,128)(2,1)S(1)} %get-tuple-element.26), channel_id=1, source_target_pairs={{0,8},{4,12},{8,0},{12,4},{16,24},{20,28},{24,16},{28,20},{1,9},{5... | collective-permute-start | bytes 196616 | tf_op jit(solution)/shard_map/ppermute | solution.py:638
  28.7 5.0 %collective-permute-start.9 = (bf16[128,256]{1,0:T(8,128)(2,1)S(1)}, bf16[128,256]{1,0:T(8,128)(2,1)S(1)}, u32[]{:S(2)}, u32[]{:S(2)}) collective-permute-start(bf16[128,256]{1,0:T(8,128)(2,1)S(1)} %get-tuple-element.21), channel_id=1, source_target_pairs={{0,16},{4,20},{8,24},{12,28},{16,0},{20,4},{24,8},{28,12},{1,17},{... | collective-permute-start | bytes 196616 | tf_op jit(solution)/shard_map/ppermute | solution.py:638
  29.6 5.2 %collective-permute-start.8 = (bf16[128,256]{1,0:T(8,128)(2,1)S(1)}, bf16[128,256]{1,0:T(8,128)(2,1)S(1)}, u32[]{:S(2)}, u32[]{:S(2)}) collective-permute-start(bf16[128,256]{1,0:T(8,128)(2,1)S(1)} %get-tuple-element.22), channel_id=1, source_target_pairs={{0,24},{4,28},{8,16},{12,20},{16,8},{20,12},{24,0},{28,4},{1,25},{... | collective-permute-start | bytes 196616 | tf_op jit(solution)/shard_map/ppermute | solution.py:638
  31.0 4.4 %collective-permute-start.10 = (bf16[128,256]{1,0:T(8,128)(2,1)S(1)}, bf16[128,256]{1,0:T(8,128)(2,1)S(1)}, u32[]{:S(2)}, u32[]{:S(2)}) collective-permute-start(bf16[128,256]{1,0:T(8,128)(2,1)S(1)} %held_block.1), channel_id=1, source_target_pairs={{0,8},{4,12},{8,0},{12,4},{16,24},{20,28},{24,16},{28,20},{1,9},{5... | collective-permute-start | bytes 196616 | tf_op jit(solution)/shard_map/ppermute | solution.py:638

commit v5 on v4

--- a/solution.py
+++ b/solution.py
@@ -404,7 +404,7 @@
     short_taps = short[:, own_lanes(width)]
     vocab = table.shape[0]
     entries = lax.broadcasted_iota(jnp.int32, (block, vocab), 1)
-    rows = 16
+    rows = 32
 
     def embed(chunk):
         for b in range(chunk * pair, (chunk + 1) * pair):
@@ -559,7 +559,10 @@
     def weigh(scores):
         peak = jnp.max(scores, axis=1, keepdims=True)
         weights = jnp.exp2((scores - peak) * (width**-0.5 * math.log2(math.e)))
-        return weights.astype(jnp.bfloat16), jnp.sum(weights, axis=1, keepdims=True)
+        folded = weights[:, :width]
+        for i in range(1, weights.shape[1] // width):
+            folded = folded + weights[:, i * width : (i + 1) * width]
+        return weights.astype(jnp.bfloat16), jnp.sum(folded, axis=1, keepdims=True)
 
     def blend(chip, side, weights, row_total):
         reach = (chip + 1) * 2 * block

time: 36.3 us -> 36.3 us (level)
  no operation moved by 1% of the time
where the time goes in v5:
time: 36.3 us; the launch traced here: 36.1 us
  starting transfers between devices  17 us (47%)
  Pallas kernels  9.77 us (27%)
  waiting for transfers between devices  8.44 us (23%)
  between operations  0.79 us (2%)
    ppermute x11, starting transfers between devices, exchange(): lax.ppermute(value, 'seq', [(i, i ^ apart) for i in range(seq_count)])  12 us
    all_to_all x1, starting transfers between devices, by_head(): all_sums = lax.all_to_all(square_sums, ('seq', 'ch'), 0, 0, tiled=True)  5.02 us
    all_to_all x1, waiting for transfers between devices, by_head(): all_sums = lax.all_to_all(square_sums, ('seq', 'ch'), 0, 0, tiled=True)  4.71 us
    pallas_call x1, Pallas kernels, by_head(): pl.pallas_call(functools.partial(conv_kernel, piece_count=len(pieces)), o...  3.74 us
    ppermute x11, waiting for transfers between devices, exchange(): lax.ppermute(value, 'seq', [(i, i ^ apart) for i in range(seq_count)])  3.73 us
    pallas_call x1, Pallas kernels, by_head(): pl.pallas_call(functools.partial(attend_kernel, channel_count=width_dev *...  1.45 us
    pallas_call x2, Pallas kernels, placed_part(): pl.pallas_call(functools.partial(place_part_kernel, order=order, extra=le...  1.36 us
    pallas_call x1, Pallas kernels, by_head(): pl.pallas_call(response_kernel, out_shape=[jax.ShapeDtypeStruct((2 * bloc...  1.34 us
  transfers between devices with their start and end apart: 12, of which 5 were waited for; matrix products, arithmetic and copies ran while one was open for 0% of the time, Pallas kernels for 15%

profile of v5, /device:TPU:0, one launch (start us, length us, event | category | flops | bytes accessed | tf_op | source)
XLA Modules:
  0.0 36.1 jit_solution(10919522119183179533)
XLA Ops:
  0.6 0.5 %collective-permute-start = (s32[128]{0:T(128)}, s32[128]{0:T(128)S(1)}, u32[]{:S(2)}, u32[]{:S(2)}) collective-permute-start(s32[128]{0:T(128)} %token_ids.1), channel_id=1, source_target_pairs={{0,4},{4,0},{8,12},{12,8},{16,20},{20,16},{24,28},{28,24},{1,5},{5... | collective-permute-start | bytes 1544 | tf_op jit(solution)/shard_map/ppermute | solution.py:641
  1.1 1.1 %fetched_operands.1 = (s32[128]{0:T(128)S(1)}, f32[16,128]{1,0:T(8,128)S(1)}, f32[16,128]{1,0:T(8,128)S(1)}, f32[128,128]{1,0:T(8,128)S(1)}, bf16[512,256]{1,0:T(8,128)(2,1)S(1)}) custom-call(s32[128]{0:T(128)} %token_ids.1, f32[16,1024]{1,0:T(8,128)} %residue.1, f32[16,1024]{1,0:T(8,128)} %rate.1, f32[128,1024]{1,0:T(8,128)} %medium.1, ...), custom_call_target="tpu_custom_call" | custom-call | flops 1000000000 | bytes 2000000 | tf_op jit(solution)/shard_map/fetched_operands/pallas_call | solution.py:651
  2.2 0.0 collective-permute-done
  2.3 3.6 %collective-permute-start.3 = (s32[2,128]{1,0:T(2,128)S(1)}, s32[2,128]{1,0:T(2,128)S(1)}, u32[]{:S(2)}, u32[]{:S(2)}) collective-permute-start(s32[2,128]{1,0:T(2,128)S(1)} %pad_add_fusion.refs_0_), channel_id=1, source_target_pairs={{0,24},{4,28},{8,16},{12,20},{16,8},{20,12},{24,0},{28,4},{1,25},{... | collective-permute-start | bytes 3080 | tf_op jit(solution)/shard_map/ppermute | solution.py:641
  5.9 0.5 %collective-permute-start.2 = (s32[2,128]{1,0:T(2,128)S(1)}, s32[2,128]{1,0:T(2,128)S(1)}, u32[]{:S(2)}, u32[]{:S(2)}) collective-permute-start(s32[2,128]{1,0:T(2,128)S(1)} %pad_add_fusion.refs_0_), channel_id=1, source_target_pairs={{0,16},{4,20},{8,24},{12,28},{16,0},{20,4},{24,8},{28,12},{1,17},{... | collective-permute-start | bytes 3080 | tf_op jit(solution)/shard_map/ppermute | solution.py:641
  6.4 0.1 collective-permute-start.1
  6.5 0.0 copy-start
  6.5 0.0 copy-start.1
  6.5 0.0 copy-start.4
  6.5 0.0 copy-start.5
  6.5 1.3 %filter_responses.1 = (f32[256,128]{1,0:T(8,128)S(1)}, f32[256,1024]{1,0:T(8,128)S(1)}) custom-call(f32[16,128]{1,0:T(8,128)S(1)} %get-tuple-element.12.residue, f32[16,128]{1,0:T(8,128)S(1)} %get-tuple-element.13.rate, f32[128,128]{1,0:T(8,128)S(1)} %get-tuple-element.14.medium, bf16[512,256]{1,0:T(8,128)(2,1)S(1)} %get-tuple-element.15.table), custom_call_target="tpu_custom_call" | custom-call | flops 2000000000 | bytes 2000000 | tf_op jit(solution)/shard_map/filter_responses/pallas_call | solution.py:669
  7.8 0.0 collective-permute-done.3.refs_3_
  7.9 1.6 %collective-permute-done.2.refs_2_ = s32[2,128]{1,0:T(2,128)S(1)} collective-permute-done((s32[2,128]{1,0:T(2,128)S(1)}, s32[2,128]{1,0:T(2,128)S(1)}, u32[]{:S(2)}, u32[]{:S(2)}) %collective-permute-start.2) | collective-permute-done | bytes 1056 | tf_op jit(solution)/shard_map/ppermute | solution.py:641
  9.4 0.5 %collective-permute-done.1.refs_1_ = s32[2,128]{1,0:T(2,128)S(1)} collective-permute-done((s32[2,128]{1,0:T(2,128)S(1)}, s32[2,128]{1,0:T(2,128)S(1)}, u32[]{:S(2)}, u32[]{:S(2)}) %collective-permute-start.1) | collective-permute-done | bytes 1056 | tf_op jit(solution)/shard_map/ppermute | solution.py:641
  9.9 0.0 copy-done
  9.9 0.0 copy-done.1
  9.9 0.0 copy-done.4
  9.9 0.0 copy-done.5
  10.0 3.7 %gated_convolutions.1 = (bf16[1024,128]{1,0:T(8,128)(2,1)S(1)}, f32[32,8,128]{2,1,0:T(8,128)}) custom-call(s32[2,128]{1,0:T(2,128)S(1)} %pad_add_fusion.refs_0_, s32[2,128]{1,0:T(2,128)S(1)} %collective-permute-done.1.refs_1_, s32[2,128]{1,0:T(2,128)S(1)} %collective-permute-done.2.refs_2_, s32[2,128]{1,0:T(2,128)S(1)} %collective-permute-done.3.refs_3_, ...), custom_call_target="tpu_custom_call" | custom-call | flops 2000000000 | bytes 2000000 | tf_op jit(solution)/shard_map/gated_convolutions/pallas_call | solution.py:683
  13.7 0.1 collective-permute-start.4
  13.8 5.0 %all-to-all-start = ((f32[32,8,128]{2,1,0:T(8,128)}), f32[32,8,128]{2,1,0:T(8,128)S(1)}, u32[]{:S(2)}, u32[]{:S(2)}) async-start(f32[32,8,128]{2,1,0:T(8,128)} %get-tuple-element.19), calls=%async_computation | async-start | bytes 262144 | tf_op jit(solution)/shard_map/all_to_all | solution.py:705
  18.8 0.0 collective-permute-done.4.other
  18.8 0.1 hyena_blocks.1
  18.9 0.0 copy-start.3
  18.9 0.0 copy-start.2
  18.9 2.7 %collective-permute-start.7 = (bf16[128,256]{1,0:T(8,128)(2,1)S(1)}, bf16[128,256]{1,0:T(8,128)(2,1)S(1)}, u32[]{:S(2)}, u32[]{:S(2)}) collective-permute-start(bf16[128,256]{1,0:T(8,128)(2,1)S(1)} %get-tuple-element.24), channel_id=1, source_target_pairs={{0,24},{4,28},{8,16},{12,20},{16,8},{20,12},{24,0},{28,4},{1,25},{... | collective-permute-start | bytes 196616 | tf_op jit(solution)/shard_map/ppermute | solution.py:641
  21.7 0.6 %collective-permute-start.6 = (bf16[128,256]{1,0:T(8,128)(2,1)S(1)}, bf16[128,256]{1,0:T(8,128)(2,1)S(1)}, u32[]{:S(2)}, u32[]{:S(2)}) collective-permute-start(bf16[128,256]{1,0:T(8,128)(2,1)S(1)} %get-tuple-element.25), channel_id=1, source_target_pairs={{0,16},{4,20},{8,24},{12,28},{16,0},{20,4},{24,8},{28,12},{1,17},{... | collective-permute-start | bytes 196616 | tf_op jit(solution)/shard_map/ppermute | solution.py:641
  22.2 0.3 collective-permute-start.5
  22.5 4.7 %all-to-all-done.sums = f32[32,8,128]{2,1,0:T(8,128)S(1)} async-done(((f32[32,8,128]{2,1,0:T(8,128)}), f32[32,8,128]{2,1,0:T(8,128)S(1)}, u32[]{:S(2)}, u32[]{:S(2)}) %all-to-all-start) | async-done | bytes 131104 | tf_op jit(solution)/shard_map/all_to_all | solution.py:705
  27.2 0.0 copy-done.3
  27.2 0.0 copy-done.2
  27.2 1.5 %attention.1 = bf16[4,128,256]{2,1,0:T(8,128)(2,1)S(1)} custom-call(bf16[1024,128]{1,0:T(8,128)(2,1)S(1)} %get-tuple-element.18.own, bf16[1024,128]{1,0:T(8,128)(2,1)S(1)} %collective-permute-done.4.other, f32[32,8,128]{2,1,0:T(8,128)S(1)} %all-to-all-done.sums, f32[1,1024]{1,0:T(1,128)S(1)} %bitcast.21, f32[1,1024]{1,0:T(1,128)S(1)} %bitcast.22), custom_call_target="tpu_custom_call" | custom-call | flops 2000000000 | bytes 1000000 | tf_op jit(solution)/shard_map/attention/pallas_call | solution.py:752
  28.7 0.9 %collective-permute-start.9 = (bf16[128,256]{1,0:T(8,128)(2,1)S(1)}, bf16[128,256]{1,0:T(8,128)(2,1)S(1)}, u32[]{:S(2)}, u32[]{:S(2)}) collective-permute-start(bf16[128,256]{1,0:T(8,128)(2,1)S(1)} %get-tuple-element.21), channel_id=1, source_target_pairs={{0,16},{4,20},{8,24},{12,28},{16,0},{20,4},{24,8},{28,12},{1,17},{... | collective-permute-start | bytes 196616 | tf_op jit(solution)/shard_map/ppermute | solution.py:641
  29.6 1.4 %collective-permute-start.8 = (bf16[128,256]{1,0:T(8,128)(2,1)S(1)}, bf16[128,256]{1,0:T(8,128)(2,1)S(1)}, u32[]{:S(2)}, u32[]{:S(2)}) collective-permute-start(bf16[128,256]{1,0:T(8,128)(2,1)S(1)} %get-tuple-element.22), channel_id=1, source_target_pairs={{0,24},{4,28},{8,16},{12,20},{16,8},{20,12},{24,0},{28,4},{1,25},{... | collective-permute-start | bytes 196616 | tf_op jit(solution)/shard_map/ppermute | solution.py:641
  31.0 0.0 collective-permute-done.7.refs_3_
  31.0 0.0 collective-permute-done.6.refs_2_
  31.0 0.0 collective-permute-done.5.refs_1_
  31.0 1.3 %collective-permute-start.10 = (bf16[128,256]{1,0:T(8,128)(2,1)S(1)}, bf16[128,256]{1,0:T(8,128)(2,1)S(1)}, u32[]{:S(2)}, u32[]{:S(2)}) collective-permute-start(bf16[128,256]{1,0:T(8,128)(2,1)S(1)} %held_block.1), channel_id=1, source_target_pairs={{0,8},{4,12},{8,0},{12,4},{16,24},{20,28},{24,16},{28,20},{1,9},{5... | collective-permute-start | bytes 196616 | tf_op jit(solution)/shard_map/ppermute | solution.py:641
  32.3 0.7 %placed_hyena.1 = bf16[128,1024]{1,0:T(8,128)(2,1)} custom-call(bf16[128,256]{1,0:T(8,128)(2,1)S(1)} %get-tuple-element.27.refs_0_, bf16[128,256]{1,0:T(8,128)(2,1)S(1)} %collective-permute-done.5.refs_1_, bf16[128,256]{1,0:T(8,128)(2,1)S(1)} %collective-permute-done.6.refs_2_, bf16[128,256]{1,0:T(8,128)(2,1)S(1)} %collective-permute-done.7.refs_3_), custom_call_target="tpu_custom_call" | custom-call | flops 1000000000 | bytes 1000000 | tf_op jit(solution)/shard_map/placed_hyena/pallas_call | solution.py:708
  33.1 0.6 %collective-permute-done.9.refs_2_ = bf16[128,256]{1,0:T(8,128)(2,1)S(1)} collective-permute-done((bf16[128,256]{1,0:T(8,128)(2,1)S(1)}, bf16[128,256]{1,0:T(8,128)(2,1)S(1)}, u32[]{:S(2)}, u32[]{:S(2)}) %collective-permute-start.9) | collective-permute-done | bytes 65568 | tf_op jit(solution)/shard_map/ppermute | solution.py:641
  33.7 1.0 %collective-permute-done.8.refs_1_ = bf16[128,256]{1,0:T(8,128)(2,1)S(1)} collective-permute-done((bf16[128,256]{1,0:T(8,128)(2,1)S(1)}, bf16[128,256]{1,0:T(8,128)(2,1)S(1)}, u32[]{:S(2)}, u32[]{:S(2)}) %collective-permute-start.8) | collective-permute-done | bytes 65568 | tf_op jit(solution)/shard_map/ppermute | solution.py:641
  34.7 0.7 %placed_early.1.refs_0_ = bf16[128,1024]{1,0:T(8,128)(2,1)} custom-call(bf16[128,256]{1,0:T(8,128)(2,1)S(1)} %get-tuple-element.23.refs_0_, bf16[128,256]{1,0:T(8,128)(2,1)S(1)} %collective-permute-done.8.refs_1_, bf16[128,256]{1,0:T(8,128)(2,1)S(1)} %collective-permute-done.9.refs_2_), custom_call_target="tpu_custom_call" | custom-call | flops 1000000000 | bytes 1000000 | tf_op jit(solution)/shard_map/placed_early/pallas_call | solution.py:719
  35.4 0.0 collective-permute-done.10.refs_1_
  35.4 0.7 %placed_attended.1 = bf16[128,1024]{1,0:T(8,128)(2,1)} custom-call(bf16[128,1024]{1,0:T(8,128)(2,1)} %placed_early.1.refs_0_, bf16[128,256]{1,0:T(8,128)(2,1)S(1)} %collective-permute-done.10.refs_1_), custom_call_target="tpu_custom_call", output_to_operand_aliasing={{}: (0, {})} | custom-call | flops 1000000000 | bytes 1000000 | tf_op jit(solution)/shard_map/placed_attended/pallas_call | solution.py:719
  (4 shorter events, 0.1 us)
Async XLA Ops:
  0.6 1.6 %collective-permute-start = (s32[128]{0:T(128)}, s32[128]{0:T(128)S(1)}, u32[]{:S(2)}, u32[]{:S(2)}) collective-permute-start(s32[128]{0:T(128)} %token_ids.1), channel_id=1, source_target_pairs={{0,4},{4,0},{8,12},{12,8},{16,20},{20,16},{24,28},{28,24},{1,5},{5... | collective-permute-start | bytes 1544 | tf_op jit(solution)/shard_map/ppermute | solution.py:641
  2.3 5.6 %collective-permute-start.3 = (s32[2,128]{1,0:T(2,128)S(1)}, s32[2,128]{1,0:T(2,128)S(1)}, u32[]{:S(2)}, u32[]{:S(2)}) collective-permute-start(s32[2,128]{1,0:T(2,128)S(1)} %pad_add_fusion.refs_0_), channel_id=1, source_target_pairs={{0,24},{4,28},{8,16},{12,20},{16,8},{20,12},{24,0},{28,4},{1,25},{... | collective-permute-start | bytes 3080 | tf_op jit(solution)/shard_map/ppermute | solution.py:641
  5.9 3.6 %collective-permute-start.2 = (s32[2,128]{1,0:T(2,128)S(1)}, s32[2,128]{1,0:T(2,128)S(1)}, u32[]{:S(2)}, u32[]{:S(2)}) collective-permute-start(s32[2,128]{1,0:T(2,128)S(1)} %pad_add_fusion.refs_0_), channel_id=1, source_target_pairs={{0,16},{4,20},{8,24},{12,28},{16,0},{20,4},{24,8},{28,12},{1,17},{... | collective-permute-start | bytes 3080 | tf_op jit(solution)/shard_map/ppermute | solution.py:641
  6.4 3.6 %collective-permute-start.1 = (s32[2,128]{1,0:T(2,128)S(1)}, s32[2,128]{1,0:T(2,128)S(1)}, u32[]{:S(2)}, u32[]{:S(2)}) collective-permute-start(s32[2,128]{1,0:T(2,128)S(1)} %pad_add_fusion.refs_0_), channel_id=1, source_target_pairs={{0,8},{4,12},{8,0},{12,4},{16,24},{20,28},{24,16},{28,20},{1,9},{5... | collective-permute-start | bytes 3080 | tf_op jit(solution)/shard_map/ppermute | solution.py:641
  6.5 3.4 %copy-start = (bf16[512,1024]{1,0:T(8,128)(2,1)S(1)}, bf16[512,1024]{1,0:T(8,128)(2,1)}, u32[]{:S(2)}) copy-start(bf16[512,1024]{1,0:T(8,128)(2,1)} %refs_4_.1) | copy-start | bytes 3145732
  6.5 3.4 %copy-start.1 = (f32[7,1024]{1,0:T(8,128)S(1)}, f32[7,1024]{1,0:T(8,128)}, u32[]{:S(2)}) copy-start(f32[7,1024]{1,0:T(8,128)} %refs_5_.1) | copy-start | bytes 86020
  6.5 3.4 %copy-start.4 = (bf16[128,1536]{1,0:T(8,128)(2,1)S(1)}, bf16[128,1536]{1,0:T(8,128)(2,1)}, u32[]{:S(2)}) copy-start(bf16[128,1536]{1,0:T(8,128)(2,1)} %constant.8.clone.refs_9_) | copy-start | bytes 1179652
  6.5 3.4 %copy-start.5 = (bf16[256,768]{1,0:T(8,128)(2,1)S(1)}, bf16[256,768]{1,0:T(8,128)(2,1)}, u32[]{:S(2)}) copy-start(bf16[256,768]{1,0:T(8,128)(2,1)} %constant.7.clone.refs_8_) | copy-start | bytes 1179652
  13.7 5.1 %collective-permute-start.4 = (bf16[1024,128]{1,0:T(8,128)(2,1)S(1)}, bf16[1024,128]{1,0:T(8,128)(2,1)S(1)}, u32[]{:S(2)}, u32[]{:S(2)}) collective-permute-start(bf16[1024,128]{1,0:T(8,128)(2,1)S(1)} %get-tuple-element.18.own), channel_id=1, source_target_pairs={{0,4},{4,0},{8,12},{12,8},{16,20},{20,16},{24,28},{28,24},{1,5},{5... | collective-permute-start | bytes 786440 | tf_op jit(solution)/shard_map/ppermute | solution.py:641
  13.8 13.4 %all-to-all-start = ((f32[32,8,128]{2,1,0:T(8,128)}), f32[32,8,128]{2,1,0:T(8,128)S(1)}, u32[]{:S(2)}, u32[]{:S(2)}) async-start(f32[32,8,128]{2,1,0:T(8,128)} %get-tuple-element.19), calls=%async_computation | async-start | bytes 262144 | tf_op jit(solution)/shard_map/all_to_all | solution.py:705
  18.9 8.3 %copy-start.3 = (f32[1024]{0:T(1024)S(1)}, f32[1024]{0:T(1024)}, u32[]{:S(2)}) copy-start(f32[1024]{0:T(1024)} %param.18) | copy-start | bytes 12292
  18.9 8.3 %copy-start.2 = (f32[1024]{0:T(1024)S(1)}, f32[1024]{0:T(1024)}, u32[]{:S(2)}) copy-start(f32[1024]{0:T(1024)} %param.17) | copy-start | bytes 12292
  18.9 12.1 %collective-permute-start.7 = (bf16[128,256]{1,0:T(8,128)(2,1)S(1)}, bf16[128,256]{1,0:T(8,128)(2,1)S(1)}, u32[]{:S(2)}, u32[]{:S(2)}) collective-permute-start(bf16[128,256]{1,0:T(8,128)(2,1)S(1)} %get-tuple-element.24), channel_id=1, source_target_pairs={{0,24},{4,28},{8,16},{12,20},{16,8},{20,12},{24,0},{28,4},{1,25},{... | collective-permute-start | bytes 196616 | tf_op jit(solution)/shard_map/ppermute | solution.py:641
  21.7 9.3 %collective-permute-start.6 = (bf16[128,256]{1,0:T(8,128)(2,1)S(1)}, bf16[128,256]{1,0:T(8,128)(2,1)S(1)}, u32[]{:S(2)}, u32[]{:S(2)}) collective-permute-start(bf16[128,256]{1,0:T(8,128)(2,1)S(1)} %get-tuple-element.25), channel_id=1, source_target_pairs={{0,16},{4,20},{8,24},{12,28},{16,0},{20,4},{24,8},{28,12},{1,17},{... | collective-permute-start | bytes 196616 | tf_op jit(solution)/shard_map/ppermute | solution.py:641
  22.2 8.8 %collective-permute-start.5 = (bf16[128,256]{1,0:T(8,128)(2,1)S(1)}, bf16[128,256]{1,0:T(8,128)(2,1)S(1)}, u32[]{:S(2)}, u32[]{:S(2)}) collective-permute-start(bf16[128,256]{1,0:T(8,128)(2,1)S(1)} %get-tuple-element.26), channel_id=1, source_target_pairs={{0,8},{4,12},{8,0},{12,4},{16,24},{20,28},{24,16},{28,20},{1,9},{5... | collective-permute-start | bytes 196616 | tf_op jit(solution)/shard_map/ppermute | solution.py:641
  28.7 5.0 %collective-permute-start.9 = (bf16[128,256]{1,0:T(8,128)(2,1)S(1)}, bf16[128,256]{1,0:T(8,128)(2,1)S(1)}, u32[]{:S(2)}, u32[]{:S(2)}) collective-permute-start(bf16[128,256]{1,0:T(8,128)(2,1)S(1)} %get-tuple-element.21), channel_id=1, source_target_pairs={{0,16},{4,20},{8,24},{12,28},{16,0},{20,4},{24,8},{28,12},{1,17},{... | collective-permute-start | bytes 196616 | tf_op jit(solution)/shard_map/ppermute | solution.py:641
  29.6 5.2 %collective-permute-start.8 = (bf16[128,256]{1,0:T(8,128)(2,1)S(1)}, bf16[128,256]{1,0:T(8,128)(2,1)S(1)}, u32[]{:S(2)}, u32[]{:S(2)}) collective-permute-start(bf16[128,256]{1,0:T(8,128)(2,1)S(1)} %get-tuple-element.22), channel_id=1, source_target_pairs={{0,24},{4,28},{8,16},{12,20},{16,8},{20,12},{24,0},{28,4},{1,25},{... | collective-permute-start | bytes 196616 | tf_op jit(solution)/shard_map/ppermute | solution.py:641
  31.0 4.4 %collective-permute-start.10 = (bf16[128,256]{1,0:T(8,128)(2,1)S(1)}, bf16[128,256]{1,0:T(8,128)(2,1)S(1)}, u32[]{:S(2)}, u32[]{:S(2)}) collective-permute-start(bf16[128,256]{1,0:T(8,128)(2,1)S(1)} %held_block.1), channel_id=1, source_target_pairs={{0,8},{4,12},{8,0},{12,4},{16,24},{20,28},{24,16},{28,20},{1,9},{5... | collective-permute-start | bytes 196616 | tf_op jit(solution)/shard_map/ppermute | solution.py:641
